TPU v7x, 512 devices: a whole 4x4x16 slice. The times are simulated.
512 devices in a mesh: ta: 4 (over z_hi), ha: 8 (over y, core), wa: 16 (over z_lo, x).
Axes of the slice: x: 4, y: 4, z: 16 (z_hi: 4, z_lo: 4; z = z_hi * 4 + z_lo), core: 2. Of those that a mesh axis runs over, the one named last changes fastest.
Arguments:
- queries: bfloat16 [24, 64, 128, 128], P('ta', 'ha', 'wa'), may hold values from -30 to 30
- keys: bfloat16 [24, 64, 128, 128], P('ta', 'ha', 'wa'), may hold values from -30 to 30
- values: bfloat16 [24, 64, 128, 128], P('ta', 'ha', 'wa'), may hold values from -6 to 6
- out_grad: bfloat16 [24, 64, 128, 128], P('ta', 'ha', 'wa'), may hold values from -6 to 6
- window_extent: int32 [4, 8, 16, 3], replicated, may hold values from 0 to 1, as said below
- pair_table: int32 [1, 27], replicated, may hold values from 0 to 1, as said below
Outputs:
- attended: bfloat16 [24, 64, 128, 128], P('ta', 'ha', 'wa')
- query_grad: bfloat16 [24, 64, 128, 128], P('ta', 'ha', 'wa')
- key_grad: bfloat16 [24, 64, 128, 128], P('ta', 'ha', 'wa')
- value_grad: bfloat16 [24, 64, 128, 128], P('ta', 'ha', 'wa')
Inputs may be any that keep to these rules, and one draw needn't show every extreme that they name: `window_extent`: at least one tile has 1 on all three axes and at least one has 0 on all three. `pair_table`: entry 13 (the tile itself) and the face offsets 4, 10, 12, 14, 16, 22 are 1 for every head.
All inputs are finite; a program needn't handle non-finite values.
Results may differ from a plain program's by a relative error of at most 0.0093.
Values may be sent and summed in bfloat16 or wider, within the bound.
No kernel may reach another device: no remote copies, remote signals or barrier semaphores. Data moves between devices by JAX's collectives and lax.ppermute only.
A program may use at most 64 MiB of HBM per device.

v0:
```python
import functools

import jax
import jax.numpy as jnp
import numpy as np
from jax import lax
from jax.experimental import pallas as pl
from jax.experimental.pallas import tpu as pltpu
from jax.sharding import PartitionSpec as P

ROWS = 384
DEPTH = 128
SCALE = DEPTH ** -0.5
LOG2E = 1.4426950408889634
SCALE2 = SCALE * LOG2E
VMEM_LIMIT = 40 * 1024 * 1024

OFFSETS = np.array(
    [[a - 1, b - 1, c - 1] for a in range(3) for b in range(3) for c in range(3)], dtype=np.int32
)
NT_DIMS = (((1,), (1,)), ((), ()))
NN_DIMS = (((1,), (0,)), ((), ()))


def swap(value, axis):
    size = lax.axis_size(axis)
    results = []
    for first in (0, 1):
        pairs = []
        for i in range(first, size - 1, 2):
            pairs += [(i, i + 1), (i + 1, i)]
        results.append(lax.ppermute(value, axis, pairs))
    return results


def allowed_slots(window_extent, pair_table):
    counts = window_extent.shape[:3]
    coords = (lax.axis_index("ta"), lax.axis_index("ha"), lax.axis_index("wa"))
    distance = jnp.abs(jnp.asarray(OFFSETS))
    inside = jnp.ones((27,), jnp.bool_)
    for axis in range(3):
        position = coords[axis] + jnp.asarray(OFFSETS[:, axis])
        inside = inside & (position >= 0) & (position < counts[axis])
    padded = jnp.pad(window_extent, ((1, 1), (1, 1), (1, 1), (0, 0)))
    near = lax.dynamic_slice(padded, coords + (jnp.int32(0),), (3, 3, 3, 3)).reshape(27, 3)
    kept = pair_table[0] == 1
    as_query = kept & inside & jnp.all(distance <= near[13][None, :], axis=1)
    as_key = kept[::-1] & inside & jnp.all(distance <= near, axis=1)
    both = jnp.stack([as_query, as_key]).astype(jnp.int32)
    place = jnp.zeros((3, 3, 3), jnp.int32)
    for axis, weight in ((0, 9), (1, 3), (2, 1)):
        sign = 1 - 2 * (coords[axis] % 2)
        shape = [1, 1, 1]
        shape[axis] = 3
        step = jnp.asarray(np.array([0, 1, -1], dtype=np.int32)) * sign + 1
        place = place + weight * step.reshape(shape)
    place = place.reshape(27)
    hot = place[:, None] == jnp.arange(27, dtype=jnp.int32)[None, :]
    slots = jnp.sum(jnp.where(hot[None], both[:, None, :], 0), axis=2).reshape(2, 3, 3, 3)
    plane = slots[:, 0].reshape(2, 9)
    rest = slots[:, 1:].transpose(0, 2, 3, 1).reshape(2, 18)
    return plane[0], rest[0], plane[1], rest[1]


def each_block(allow_ref, stacks, count, step):
    for part in range(3):
        def body(i, carry, part=part):
            @pl.when(allow_ref[part * count + i] == 1)
            def _():
                step(stacks[part], i)
            return carry
        lax.fori_loop(0, count, body, 0)


def forward_step(q_ref, peak, total, acc, stack, i):
    scores = lax.dot_general(q_ref[...], stack[i, 0], NT_DIMS, preferred_element_type=jnp.float32)
    old = peak[:, :1]
    new = jnp.maximum(old, jnp.max(scores, axis=1, keepdims=True))
    chance = jnp.exp2((scores - new) * SCALE2)
    shrink = jnp.exp2((old - new) * SCALE2)
    total[:, :1] = total[:, :1] * shrink + jnp.sum(chance, axis=1, keepdims=True)
    peak[:, :1] = new
    mixed = lax.dot_general(
        chance.astype(jnp.bfloat16), stack[i, 1], NN_DIMS, preferred_element_type=jnp.float32
    )
    acc[...] = acc[...] * shrink + mixed


def forward_first(allow_ref, q_ref, s0, s1, s2, peak, total, acc):
    peak[...] = jnp.full(peak.shape, -1e30, jnp.float32)
    total[...] = jnp.zeros(total.shape, jnp.float32)
    acc[...] = jnp.zeros(acc.shape, jnp.float32)
    each_block(allow_ref, (s0, s1, s2), 3, functools.partial(forward_step, q_ref, peak, total, acc))


def forward_last(
    allow_ref, q_ref, g_ref, s0, s1, s2, peak_in, total_in, acc_in,
    out_ref, rows_ref, cols_ref, peak, total, acc,
):
    peak[...] = peak_in[...]
    total[...] = total_in[...]
    acc[...] = acc_in[...]
    each_block(allow_ref, (s0, s1, s2), 6, functools.partial(forward_step, q_ref, peak, total, acc))
    mixed = acc[...] / total[:, :1]
    out_ref[...] = mixed.astype(out_ref.dtype)
    delta = jnp.sum(mixed * g_ref[...].astype(jnp.float32), axis=1, keepdims=True)
    norm = peak[:, :1] * SCALE2 + jnp.log2(total[:, :1])
    lane = lax.broadcasted_iota(jnp.int32, (ROWS, DEPTH), 1)
    cols = jnp.where(lane == 0, norm, delta)
    cols_ref[...] = cols
    rows_ref[...] = cols.T[:8]


def query_side(
    allow0, allow1, q_ref, g_ref, cols_ref, a0, a1, a2, b0, b1, b2, out_ref, acc
):
    acc[...] = jnp.zeros(acc.shape, jnp.float32)

    def step(stack, i):
        key, value = stack[i, 0], stack[i, 1]
        scores = lax.dot_general(q_ref[...], key, NT_DIMS, preferred_element_type=jnp.float32)
        chance = jnp.exp2(scores * SCALE2 - cols_ref[:, :1])
        grad_chance = lax.dot_general(g_ref[...], value, NT_DIMS, preferred_element_type=jnp.float32)
        grad_score = (chance * (grad_chance - cols_ref[:, 1:2]) * SCALE).astype(jnp.bfloat16)
        acc[...] += lax.dot_general(grad_score, key, NN_DIMS, preferred_element_type=jnp.float32)

    each_block(allow0, (a0, a1, a2), 3, step)
    each_block(allow1, (b0, b1, b2), 6, step)
    out_ref[...] = acc[...].astype(out_ref.dtype)


def key_side(count, finish, allow_ref, k_ref, v_ref, s0, s1, s2, r0, r1, r2, *rest):
    if finish:
        key_in, value_in, key_out, value_out, key_acc, value_acc = rest
        key_acc[...] = key_in[...]
        value_acc[...] = value_in[...]
    else:
        key_acc, value_acc = rest
        key_acc[...] = jnp.zeros(key_acc.shape, jnp.float32)
        value_acc[...] = jnp.zeros(value_acc.shape, jnp.float32)

    def step(refs, i):
        stack, rows = refs
        query, grad = stack[i, 0], stack[i, 1]
        stat = rows[i]
        scores = lax.dot_general(k_ref[...], query, NT_DIMS, preferred_element_type=jnp.float32)
        chance = jnp.exp2(scores * SCALE2 - stat[0:1, :])
        grad_chance = lax.dot_general(v_ref[...], grad, NT_DIMS, preferred_element_type=jnp.float32)
        grad_score = (chance * (grad_chance - stat[1:2, :]) * SCALE).astype(jnp.bfloat16)
        key_acc[...] += lax.dot_general(grad_score, query, NN_DIMS, preferred_element_type=jnp.float32)
        value_acc[...] += lax.dot_general(
            chance.astype(jnp.bfloat16), grad, NN_DIMS, preferred_element_type=jnp.float32
        )

    each_block(allow_ref, ((s0, r0), (s1, r1), (s2, r2)), count, step)
    if finish:
        key_out[...] = key_acc[...].astype(key_out.dtype)
        value_out[...] = value_acc[...].astype(value_out.dtype)


def call(kernel, name, in_smem, out_shape, scratch=(), blocks=9):
    smem = pl.BlockSpec(memory_space=pltpu.SMEM)
    vmem = pl.BlockSpec(memory_space=pltpu.VMEM)
    area = blocks * ROWS * ROWS

    def run(*operands):
        return pl.pallas_call(
            kernel,
            out_shape=out_shape,
            in_specs=[smem if i < in_smem else vmem for i in range(len(operands))],
            out_specs=jax.tree.map(lambda _: vmem, out_shape),
            scratch_shapes=list(scratch),
            compiler_params=pltpu.CompilerParams(vmem_limit_bytes=VMEM_LIMIT),
            cost_estimate=pl.CostEstimate(
                flops=area * DEPTH * 8, transcendentals=area, bytes_accessed=blocks * ROWS * DEPTH * 4
            ),
            name=name,
        )(*operands)

    return run


def halo_first(own):
    first = jnp.stack([own] + swap(own, "wa"))
    return [first] + swap(first, "ha")


def halo_rest(own):
    planes = jnp.stack(swap(own, "ta"))
    row = jnp.concatenate([planes] + swap(planes, "wa"))
    return [row] + swap(row, "ha")


def on_device(queries, keys, values, out_grad, window_extent, pair_table):
    out_block = queries.shape
    q, k, v, g = (x.reshape(ROWS, DEPTH) for x in (queries, keys, values, out_grad))
    query0, query1, key0, key1 = allowed_slots(window_extent, pair_table)
    wide = jax.ShapeDtypeStruct((ROWS, DEPTH), jnp.float32)
    narrow = jax.ShapeDtypeStruct((ROWS, DEPTH), jnp.bfloat16)
    wide_scratch = pltpu.VMEM((ROWS, DEPTH), jnp.float32)
    rows_shape = jax.ShapeDtypeStruct((8, ROWS), jnp.float32)

    kv = jnp.stack([k, v])
    qg = jnp.stack([q, g])
    kv0 = halo_first(kv)
    kv1 = halo_rest(kv)
    qg0 = halo_first(qg)
    qg1 = halo_rest(qg)

    state = call(forward_first, "forward_first", 1, (wide, wide, wide))(query0, q, *kv0)
    attended, rows, cols = call(
        forward_last, "forward_last", 1, (narrow, rows_shape, wide), [wide_scratch] * 3, 18
    )(query1, q, g, *kv1, *state)
    rows0 = halo_first(rows)
    rows1 = halo_rest(rows)
    query_grad = call(query_side, "query_side", 2, narrow, [wide_scratch], 27)(
        query0, query1, q, g, cols, *kv0, *kv1
    )
    partial = call(functools.partial(key_side, 3, False), "key_first", 1, (wide, wide))(
        key0, k, v, *qg0, *rows0
    )
    key_grad, value_grad = call(
        functools.partial(key_side, 6, True), "key_last", 1, (narrow, narrow), [wide_scratch] * 2, 18
    )(key1, k, v, *qg1, *rows1, *partial)
    return tuple(x.reshape(out_block) for x in (attended, query_grad, key_grad, value_grad))


def solution(mesh):
    split = P("ta", "ha", "wa", None)
    return jax.shard_map(
        on_device,
        mesh=mesh,
        in_specs=(split, split, split, split, P(), P()),
        out_specs=(split, split, split, split),
        check_vma=False,
    )
```

profile of v0, /device:TPU:7, one launch (start us, length us, event | category | flops | bytes accessed | tf_op | source)
XLA Modules:
  0.0 171.4 jit_solution(5970289765919648433)
XLA Ops:
  2.4 17.0 %collective-permute-start = (bf16[2,384,128]{2,1,0:T(8,128)(2,1)S(1)}, bf16[2,384,128]{2,1,0:T(8,128)(2,1)S(1)}, u32[]{:S(2)}, u32[]{:S(2)}) collective-permute-start(bf16[2,384,128]{2,1,0:T(8,128)(2,1)S(1)} %get-tuple-element.31), channel_id=1, source_target_pairs={{0,128},{128,0},{256,384},{384,256},{1,129},{129,1},{257,385},{385... | collective-permute-start | bytes 589832 | tf_op jit(solution)/shard_map/ppermute | solution.py:32
  19.4 2.6 %collective-permute-start.7 = (bf16[2,384,128]{2,1,0:T(8,128)(2,1)S(1)}, bf16[2,384,128]{2,1,0:T(8,128)(2,1)S(1)}, u32[]{:S(2)}, u32[]{:S(2)}) collective-permute-start(bf16[2,384,128]{2,1,0:T(8,128)(2,1)S(1)} %get-tuple-element.31), channel_id=1, source_target_pairs={{1,2},{2,1},{3,4},{4,3},{5,6},{6,5},{7,8},{8,7},{9,10},{10,9},{11,... | collective-permute-start | bytes 589832 | tf_op jit(solution)/shard_map/ppermute | solution.py:32
  24.3 4.0 %collective-permute-start.10 = (bf16[2,384,128]{2,1,0:T(8,128)(2,1)}, bf16[2,384,128]{2,1,0:T(8,128)(2,1)S(1)}, u32[]{:S(2)}, u32[]{:S(2)}) collective-permute-start(bf16[2,384,128]{2,1,0:T(8,128)(2,1)} %get-tuple-element.29), channel_id=1, source_target_pairs={{0,128},{128,0},{256,384},{384,256},{1,129},{129,1},{257,385},{385... | collective-permute-start | bytes 589832 | tf_op jit(solution)/shard_map/ppermute | solution.py:32
  29.3 18.3 %collective-permute-done = bf16[2,384,128]{2,1,0:T(8,128)(2,1)S(1)} collective-permute-done((bf16[2,384,128]{2,1,0:T(8,128)(2,1)S(1)}, bf16[2,384,128]{2,1,0:T(8,128)(2,1)S(1)}, u32[]{:S(2)}, u32[]{:S(2)}) %collective-permute-start) | collective-permute-done | bytes 196640 | tf_op jit(solution)/shard_map/ppermute | solution.py:32
  49.6 2.3 %collective-permute-start.2 = (bf16[2,2,384,128]{3,2,1,0:T(8,128)(2,1)S(1)}, bf16[2,2,384,128]{3,2,1,0:T(8,128)(2,1)S(1)}, u32[]{:S(2)}, u32[]{:S(2)}) collective-permute-start(bf16[2,2,384,128]{3,2,1,0:T(8,128)(2,1)S(1)} %pad_maximum_fusion.4), channel_id=1, source_target_pairs={{0,1},{1,0},{2,3},{3,2},{4,5},{5,4},{6,7},{7,6},{8,9},{9,8},{10,11... | collective-permute-start | bytes 1179656 | tf_op jit(solution)/shard_map/ppermute | solution.py:32
  52.6 3.0 %collective-permute-start.6 = (bf16[2,384,128]{2,1,0:T(8,128)(2,1)S(1)}, bf16[2,384,128]{2,1,0:T(8,128)(2,1)S(1)}, u32[]{:S(2)}, u32[]{:S(2)}) collective-permute-start(bf16[2,384,128]{2,1,0:T(8,128)(2,1)S(1)} %get-tuple-element.31), channel_id=1, source_target_pairs={{0,1},{1,0},{2,3},{3,2},{4,5},{5,4},{6,7},{7,6},{8,9},{9,8},{10,11... | collective-permute-start | bytes 589832 | tf_op jit(solution)/shard_map/ppermute | solution.py:32
  55.7 5.5 %collective-permute-start.23 = (bf16[2,384,128]{2,1,0:T(8,128)(2,1)}, bf16[2,384,128]{2,1,0:T(8,128)(2,1)S(1)}, u32[]{:S(2)}, u32[]{:S(2)}) collective-permute-start(bf16[2,384,128]{2,1,0:T(8,128)(2,1)} %get-tuple-element.29), channel_id=1, source_target_pairs={{1,2},{2,1},{3,4},{4,3},{5,6},{6,5},{7,8},{8,7},{9,10},{10,9},{11,... | collective-permute-start | bytes 589832 | tf_op jit(solution)/shard_map/ppermute | solution.py:32
  63.1 2.6 %collective-permute-start.13 = (bf16[2,2,384,128]{3,2,1,0:T(8,128)(2,1)S(1)}, bf16[2,2,384,128]{3,2,1,0:T(8,128)(2,1)S(1)}, u32[]{:S(2)}, u32[]{:S(2)}) collective-permute-start(bf16[2,2,384,128]{3,2,1,0:T(8,128)(2,1)S(1)} %pad_maximum_fusion.5), channel_id=1, source_target_pairs={{1,2},{2,1},{3,4},{4,3},{5,6},{6,5},{7,8},{8,7},{9,10},{10,9},{11,... | collective-permute-start | bytes 1179656 | tf_op jit(solution)/shard_map/ppermute | solution.py:32
  65.9 7.4 %collective-permute-start.4 = (bf16[6,2,384,128]{3,2,1,0:T(8,128)(2,1)S(1)}, bf16[6,2,384,128]{3,2,1,0:T(8,128)(2,1)S(1)}, u32[]{:S(2)}, u32[]{:S(2)}) collective-permute-start(bf16[6,2,384,128]{3,2,1,0:T(8,128)(2,1)S(1)} %pad_maximum_fusion.s0.b0), channel_id=1, source_target_pairs={{0,16},{16,0},{32,48},{48,32},{64,80},{80,64},{96,112},{112,96},{1... | collective-permute-start | bytes 3538952 | tf_op jit(solution)/shard_map/ppermute | solution.py:32
  73.3 3.1 %collective-permute-start.5 = (bf16[6,2,384,128]{3,2,1,0:T(8,128)(2,1)S(1)}, bf16[6,2,384,128]{3,2,1,0:T(8,128)(2,1)}, u32[]{:S(2)}, u32[]{:S(2)}) collective-permute-start(bf16[6,2,384,128]{3,2,1,0:T(8,128)(2,1)S(1)} %pad_maximum_fusion.s0.b0), channel_id=1, source_target_pairs={{16,32},{32,16},{48,64},{64,48},{80,96},{96,80},{17,33},{33,17},{4... | collective-permute-start | bytes 3538952 | tf_op jit(solution)/shard_map/ppermute | solution.py:32
  81.3 3.6 %collective-permute-start.9 = (bf16[3,2,384,128]{3,2,1,0:T(8,128)(2,1)S(1)}, bf16[3,2,384,128]{3,2,1,0:T(8,128)(2,1)}, u32[]{:S(2)}, u32[]{:S(2)}) collective-permute-start(bf16[3,2,384,128]{3,2,1,0:T(8,128)(2,1)S(1)} %pad_maximum_fusion.2.s0.a0), channel_id=1, source_target_pairs={{16,32},{32,16},{48,64},{64,48},{80,96},{96,80},{17,33},{33,17},{4... | collective-permute-start | bytes 1769480 | tf_op jit(solution)/shard_map/ppermute | solution.py:32
  85.1 3.3 %collective-permute-done.12 = bf16[2,2,384,128]{3,2,1,0:T(8,128)(2,1)} collective-permute-done((bf16[2,2,384,128]{3,2,1,0:T(8,128)(2,1)S(1)}, bf16[2,2,384,128]{3,2,1,0:T(8,128)(2,1)}, u32[]{:S(2)}, u32[]{:S(2)}) %collective-permute-start.12) | collective-permute-done | bytes 393248 | tf_op jit(solution)/shard_map/ppermute | solution.py:32
  97.4 2.4 %collective-permute-start.14 = (bf16[6,2,384,128]{3,2,1,0:T(8,128)(2,1)S(1)}, bf16[6,2,384,128]{3,2,1,0:T(8,128)(2,1)S(1)}, u32[]{:S(2)}, u32[]{:S(2)}) collective-permute-start(bf16[6,2,384,128]{3,2,1,0:T(8,128)(2,1)S(1)} %pad_maximum_fusion.1.s0), channel_id=1, source_target_pairs={{0,16},{16,0},{32,48},{48,32},{64,80},{80,64},{96,112},{112,96},{1... | collective-permute-start | bytes 3538952 | tf_op jit(solution)/shard_map/ppermute | solution.py:32
  99.8 4.4 %collective-permute-start.15 = (bf16[6,2,384,128]{3,2,1,0:T(8,128)(2,1)S(1)}, bf16[6,2,384,128]{3,2,1,0:T(8,128)(2,1)S(1)}, u32[]{:S(2)}, u32[]{:S(2)}) collective-permute-start(bf16[6,2,384,128]{3,2,1,0:T(8,128)(2,1)S(1)} %pad_maximum_fusion.1.s0), channel_id=1, source_target_pairs={{16,32},{32,16},{48,64},{64,48},{80,96},{96,80},{17,33},{33,17},{4... | collective-permute-start | bytes 3538952 | tf_op jit(solution)/shard_map/ppermute | solution.py:32
  104.3 6.2 %forward_first.1 = (f32[384,128]{1,0:T(8,128)S(1)}, f32[384,128]{1,0:T(8,128)S(1)}, f32[384,128]{1,0:T(8,128)S(1)}) custom-call(s32[9]{0:T(128)S(1)} %squeeze.14.allow_ref.allow0, bf16[384,128]{1,0:T(8,128)(2,1)S(1)} %bitcast.42, bf16[3,2,384,128]{3,2,1,0:T(8,128)(2,1)S(1)} %pad_maximum_fusion.2.s0.a0, ...), custom_call_target="tpu_custom_call" | custom-call | flops 1358954496 | bytes 1769472 | tf_op jit(solution)/shard_map/forward_first/pallas_call | solution.py:167
  112.4 5.6 %forward_last.1 = (bf16[384,128]{1,0:T(8,128)(2,1)}, f32[8,384]{1,0:T(8,128)S(1)}, f32[384,128]{1,0:T(8,128)S(1)}) custom-call(s32[18]{0:T(128)S(1)} %squeeze.13.allow_ref.allow1, bf16[384,128]{1,0:T(8,128)(2,1)S(1)} %bitcast.43, bf16[384,128]{1,0:T(8,128)(2,1)S(1)} %bitcast.46, bf16[6,2,384,128]{3,2,1,0:T(8,128)(2,1)S(1)} %pad_maximum_fusion.s0.b0, ...), custom_call_target="tpu_custom_call" | custom-call | flops 2717908992 | bytes 3538944 | tf_op jit(solution)/shard_map/forward_last/pallas_call | solution.py:167
  118.6 13.7 %collective-permute-start.16 = (f32[8,384]{1,0:T(8,128)S(1)}, f32[8,384]{1,0:T(8,128)S(1)}, u32[]{:S(2)}, u32[]{:S(2)}) collective-permute-start(f32[8,384]{1,0:T(8,128)S(1)} %get-tuple-element.19), channel_id=1, source_target_pairs={{0,128},{128,0},{256,384},{384,256},{1,129},{129,1},{257,385},{385... | collective-permute-start | bytes 36872 | tf_op jit(solution)/shard_map/ppermute | solution.py:32
  132.4 7.7 %query_side.1 = bf16[384,128]{1,0:T(8,128)(2,1)} custom-call(s32[9]{0:T(128)S(1)} %squeeze.14.allow_ref.allow0, s32[18]{0:T(128)S(1)} %squeeze.13.allow_ref.allow1, bf16[384,128]{1,0:T(8,128)(2,1)S(1)} %bitcast.44, bf16[384,128]{1,0:T(8,128)(2,1)S(1)} %bitcast.47, f32[384,128]{1,0:T(8,128)S(1)} %get-tuple-element.18.cols_ref, ...), custom_call_target="tpu_custom_call" | custom-call | flops 4076863488 | bytes 5308416 | tf_op jit(solution)/shard_map/query_side/pallas_call | solution.py:167
  140.1 2.4 %collective-permute-start.27 = (f32[8,384]{1,0:T(8,128)S(1)}, f32[8,384]{1,0:T(8,128)S(1)}, u32[]{:S(2)}, u32[]{:S(2)}) collective-permute-start(f32[8,384]{1,0:T(8,128)S(1)} %get-tuple-element.19), channel_id=1, source_target_pairs={{1,2},{2,1},{3,4},{4,3},{5,6},{6,5},{7,8},{8,7},{9,10},{10,9},{11,... | collective-permute-start | bytes 36872 | tf_op jit(solution)/shard_map/ppermute | solution.py:32
  146.7 2.8 %collective-permute-start.19 = (f32[2,8,384]{2,1,0:T(8,128)S(1)}, f32[2,8,384]{2,1,0:T(8,128)S(1)}, u32[]{:S(2)}, u32[]{:S(2)}) collective-permute-start(f32[2,8,384]{2,1,0:T(8,128)S(1)} %pad_maximum_fusion.10), channel_id=1, source_target_pairs={{1,2},{2,1},{3,4},{4,3},{5,6},{6,5},{7,8},{8,7},{9,10},{10,9},{11,... | collective-permute-start | bytes 73736 | tf_op jit(solution)/shard_map/ppermute | solution.py:32
  155.3 4.5 %collective-permute-start.29 = (f32[3,8,384]{2,1,0:T(8,128)S(1)}, f32[3,8,384]{2,1,0:T(8,128)S(1)}, u32[]{:S(2)}, u32[]{:S(2)}) collective-permute-start(f32[3,8,384]{2,1,0:T(8,128)S(1)} %pad_maximum_fusion.9.r0), channel_id=1, source_target_pairs={{16,32},{32,16},{48,64},{64,48},{80,96},{96,80},{17,33},{33,17},{4... | collective-permute-start | bytes 110600 | tf_op jit(solution)/shard_map/ppermute | solution.py:32
  161.7 2.6 %collective-permute-start.21 = (f32[6,8,384]{2,1,0:T(8,128)S(1)}, f32[6,8,384]{2,1,0:T(8,128)S(1)}, u32[]{:S(2)}, u32[]{:S(2)}) collective-permute-start(f32[6,8,384]{2,1,0:T(8,128)S(1)} %pad_maximum_fusion.8.r0), channel_id=1, source_target_pairs={{16,32},{32,16},{48,64},{64,48},{80,96},{96,80},{17,33},{33,17},{4... | collective-permute-start | bytes 221192 | tf_op jit(solution)/shard_map/ppermute | solution.py:32
  164.3 3.9 %key_first.1 = (f32[384,128]{1,0:T(8,128)S(1)}, f32[384,128]{1,0:T(8,128)S(1)}) custom-call(s32[9]{0:T(128)S(1)} %squeeze.16.allow_ref, bf16[384,128]{1,0:T(8,128)(2,1)S(1)} %bitcast.52, bf16[384,128]{1,0:T(8,128)(2,1)S(1)} %bitcast.49, bf16[3,2,384,128]{3,2,1,0:T(8,128)(2,1)S(1)} %pad_maximum_fusion.3.s0, ...), custom_call_target="tpu_custom_call" | custom-call | flops 1358954496 | bytes 1769472 | tf_op jit(solution)/shard_map/key_first/pallas_call | solution.py:167
  168.3 3.1 %key_last.1 = (bf16[384,128]{1,0:T(8,128)(2,1)}, bf16[384,128]{1,0:T(8,128)(2,1)}) custom-call(s32[18]{0:T(128)S(1)} %squeeze.15.allow_ref, bf16[384,128]{1,0:T(8,128)(2,1)S(1)} %bitcast.53, bf16[384,128]{1,0:T(8,128)(2,1)S(1)} %bitcast.50, bf16[6,2,384,128]{3,2,1,0:T(8,128)(2,1)S(1)} %pad_maximum_fusion.1.s0, ...), custom_call_target="tpu_custom_call" | custom-call | flops 2717908992 | bytes 3538944 | tf_op jit(solution)/shard_map/key_last/pallas_call | solution.py:167
  (112 shorter events, 38.1 us)
Async XLA Ops:
  1.7 27.6 %collective-permute-start.1 = (bf16[2,384,128]{2,1,0:T(8,128)(2,1)S(1)}, bf16[2,384,128]{2,1,0:T(8,128)(2,1)S(1)}, u32[]{:S(2)}, u32[]{:S(2)}) collective-permute-start(bf16[2,384,128]{2,1,0:T(8,128)(2,1)S(1)} %get-tuple-element.31), channel_id=1, source_target_pairs={{128,256},{256,128},{129,257},{257,129},{130,258},{258,130},{131,2... | collective-permute-start | bytes 589832 | tf_op jit(solution)/shard_map/ppermute | solution.py:32
  2.4 45.2 %collective-permute-start = (bf16[2,384,128]{2,1,0:T(8,128)(2,1)S(1)}, bf16[2,384,128]{2,1,0:T(8,128)(2,1)S(1)}, u32[]{:S(2)}, u32[]{:S(2)}) collective-permute-start(bf16[2,384,128]{2,1,0:T(8,128)(2,1)S(1)} %get-tuple-element.31), channel_id=1, source_target_pairs={{0,128},{128,0},{256,384},{384,256},{1,129},{129,1},{257,385},{385... | collective-permute-start | bytes 589832 | tf_op jit(solution)/shard_map/ppermute | solution.py:32
  19.4 46.5 %collective-permute-start.7 = (bf16[2,384,128]{2,1,0:T(8,128)(2,1)S(1)}, bf16[2,384,128]{2,1,0:T(8,128)(2,1)S(1)}, u32[]{:S(2)}, u32[]{:S(2)}) collective-permute-start(bf16[2,384,128]{2,1,0:T(8,128)(2,1)S(1)} %get-tuple-element.31), channel_id=1, source_target_pairs={{1,2},{2,1},{3,4},{4,3},{5,6},{6,5},{7,8},{8,7},{9,10},{10,9},{11,... | collective-permute-start | bytes 589832 | tf_op jit(solution)/shard_map/ppermute | solution.py:32
  23.7 28.9 %collective-permute-start.11 = (bf16[2,384,128]{2,1,0:T(8,128)(2,1)}, bf16[2,384,128]{2,1,0:T(8,128)(2,1)S(1)}, u32[]{:S(2)}, u32[]{:S(2)}) collective-permute-start(bf16[2,384,128]{2,1,0:T(8,128)(2,1)} %get-tuple-element.29), channel_id=1, source_target_pairs={{128,256},{256,128},{129,257},{257,129},{130,258},{258,130},{131,2... | collective-permute-start | bytes 589832 | tf_op jit(solution)/shard_map/ppermute | solution.py:32
  24.3 31.3 %collective-permute-start.10 = (bf16[2,384,128]{2,1,0:T(8,128)(2,1)}, bf16[2,384,128]{2,1,0:T(8,128)(2,1)S(1)}, u32[]{:S(2)}, u32[]{:S(2)}) collective-permute-start(bf16[2,384,128]{2,1,0:T(8,128)(2,1)} %get-tuple-element.29), channel_id=1, source_target_pairs={{0,128},{128,0},{256,384},{384,256},{1,129},{129,1},{257,385},{385... | collective-permute-start | bytes 589832 | tf_op jit(solution)/shard_map/ppermute | solution.py:32
  47.6 13.6 %collective-permute-start.3 = (bf16[2,2,384,128]{3,2,1,0:T(8,128)(2,1)S(1)}, bf16[2,2,384,128]{3,2,1,0:T(8,128)(2,1)S(1)}, u32[]{:S(2)}, u32[]{:S(2)}) collective-permute-start(bf16[2,2,384,128]{3,2,1,0:T(8,128)(2,1)S(1)} %pad_maximum_fusion.4), channel_id=1, source_target_pairs={{1,2},{2,1},{3,4},{4,3},{5,6},{6,5},{7,8},{8,7},{9,10},{10,9},{11,... | collective-permute-start | bytes 1179656 | tf_op jit(solution)/shard_map/ppermute | solution.py:32
  49.6 13.6 %collective-permute-start.2 = (bf16[2,2,384,128]{3,2,1,0:T(8,128)(2,1)S(1)}, bf16[2,2,384,128]{3,2,1,0:T(8,128)(2,1)S(1)}, u32[]{:S(2)}, u32[]{:S(2)}) collective-permute-start(bf16[2,2,384,128]{3,2,1,0:T(8,128)(2,1)S(1)} %pad_maximum_fusion.4), channel_id=1, source_target_pairs={{0,1},{1,0},{2,3},{3,2},{4,5},{5,4},{6,7},{7,6},{8,9},{9,8},{10,11... | collective-permute-start | bytes 1179656 | tf_op jit(solution)/shard_map/ppermute | solution.py:32
  52.6 20.7 %collective-permute-start.6 = (bf16[2,384,128]{2,1,0:T(8,128)(2,1)S(1)}, bf16[2,384,128]{2,1,0:T(8,128)(2,1)S(1)}, u32[]{:S(2)}, u32[]{:S(2)}) collective-permute-start(bf16[2,384,128]{2,1,0:T(8,128)(2,1)S(1)} %get-tuple-element.31), channel_id=1, source_target_pairs={{0,1},{1,0},{2,3},{3,2},{4,5},{5,4},{6,7},{7,6},{8,9},{9,8},{10,11... | collective-permute-start | bytes 589832 | tf_op jit(solution)/shard_map/ppermute | solution.py:32
  55.7 20.8 %collective-permute-start.23 = (bf16[2,384,128]{2,1,0:T(8,128)(2,1)}, bf16[2,384,128]{2,1,0:T(8,128)(2,1)S(1)}, u32[]{:S(2)}, u32[]{:S(2)}) collective-permute-start(bf16[2,384,128]{2,1,0:T(8,128)(2,1)} %get-tuple-element.29), channel_id=1, source_target_pairs={{1,2},{2,1},{3,4},{4,3},{5,6},{6,5},{7,8},{8,7},{9,10},{10,9},{11,... | collective-permute-start | bytes 589832 | tf_op jit(solution)/shard_map/ppermute | solution.py:32
  61.2 18.2 %collective-permute-start.22 = (bf16[2,384,128]{2,1,0:T(8,128)(2,1)}, bf16[2,384,128]{2,1,0:T(8,128)(2,1)S(1)}, u32[]{:S(2)}, u32[]{:S(2)}) collective-permute-start(bf16[2,384,128]{2,1,0:T(8,128)(2,1)} %get-tuple-element.29), channel_id=1, source_target_pairs={{0,1},{1,0},{2,3},{3,2},{4,5},{5,4},{6,7},{7,6},{8,9},{9,8},{10,11... | collective-permute-start | bytes 589832 | tf_op jit(solution)/shard_map/ppermute | solution.py:32
  63.1 18.2 %collective-permute-start.13 = (bf16[2,2,384,128]{3,2,1,0:T(8,128)(2,1)S(1)}, bf16[2,2,384,128]{3,2,1,0:T(8,128)(2,1)S(1)}, u32[]{:S(2)}, u32[]{:S(2)}) collective-permute-start(bf16[2,2,384,128]{3,2,1,0:T(8,128)(2,1)S(1)} %pad_maximum_fusion.5), channel_id=1, source_target_pairs={{1,2},{2,1},{3,4},{4,3},{5,6},{6,5},{7,8},{8,7},{9,10},{10,9},{11,... | collective-permute-start | bytes 1179656 | tf_op jit(solution)/shard_map/ppermute | solution.py:32
  65.9 44.5 %collective-permute-start.4 = (bf16[6,2,384,128]{3,2,1,0:T(8,128)(2,1)S(1)}, bf16[6,2,384,128]{3,2,1,0:T(8,128)(2,1)S(1)}, u32[]{:S(2)}, u32[]{:S(2)}) collective-permute-start(bf16[6,2,384,128]{3,2,1,0:T(8,128)(2,1)S(1)} %pad_maximum_fusion.s0.b0), channel_id=1, source_target_pairs={{0,16},{16,0},{32,48},{48,32},{64,80},{80,64},{96,112},{112,96},{1... | collective-permute-start | bytes 3538952 | tf_op jit(solution)/shard_map/ppermute | solution.py:32
  73.3 39.1 %collective-permute-start.5 = (bf16[6,2,384,128]{3,2,1,0:T(8,128)(2,1)S(1)}, bf16[6,2,384,128]{3,2,1,0:T(8,128)(2,1)}, u32[]{:S(2)}, u32[]{:S(2)}) collective-permute-start(bf16[6,2,384,128]{3,2,1,0:T(8,128)(2,1)S(1)} %pad_maximum_fusion.s0.b0), channel_id=1, source_target_pairs={{16,32},{32,16},{48,64},{64,48},{80,96},{96,80},{17,33},{33,17},{4... | collective-permute-start | bytes 3538952 | tf_op jit(solution)/shard_map/ppermute | solution.py:32
  76.5 11.9 %collective-permute-start.12 = (bf16[2,2,384,128]{3,2,1,0:T(8,128)(2,1)S(1)}, bf16[2,2,384,128]{3,2,1,0:T(8,128)(2,1)}, u32[]{:S(2)}, u32[]{:S(2)}) collective-permute-start(bf16[2,2,384,128]{3,2,1,0:T(8,128)(2,1)S(1)} %pad_maximum_fusion.5), channel_id=1, source_target_pairs={{0,1},{1,0},{2,3},{3,2},{4,5},{5,4},{6,7},{7,6},{8,9},{9,8},{10,11... | collective-permute-start | bytes 1179656 | tf_op jit(solution)/shard_map/ppermute | solution.py:32
  79.4 18.0 %collective-permute-start.8 = (bf16[3,2,384,128]{3,2,1,0:T(8,128)(2,1)S(1)}, bf16[3,2,384,128]{3,2,1,0:T(8,128)(2,1)}, u32[]{:S(2)}, u32[]{:S(2)}) collective-permute-start(bf16[3,2,384,128]{3,2,1,0:T(8,128)(2,1)S(1)} %pad_maximum_fusion.2.s0.a0), channel_id=1, source_target_pairs={{0,16},{16,0},{32,48},{48,32},{64,80},{80,64},{96,112},{112,96},{1... | collective-permute-start | bytes 1769480 | tf_op jit(solution)/shard_map/ppermute | solution.py:32
  81.3 18.5 %collective-permute-start.9 = (bf16[3,2,384,128]{3,2,1,0:T(8,128)(2,1)S(1)}, bf16[3,2,384,128]{3,2,1,0:T(8,128)(2,1)}, u32[]{:S(2)}, u32[]{:S(2)}) collective-permute-start(bf16[3,2,384,128]{3,2,1,0:T(8,128)(2,1)S(1)} %pad_maximum_fusion.2.s0.a0), channel_id=1, source_target_pairs={{16,32},{32,16},{48,64},{64,48},{80,96},{96,80},{17,33},{33,17},{4... | collective-permute-start | bytes 1769480 | tf_op jit(solution)/shard_map/ppermute | solution.py:32
  88.3 30.3 %collective-permute-start.24 = (bf16[3,2,384,128]{3,2,1,0:T(8,128)(2,1)S(1)}, bf16[3,2,384,128]{3,2,1,0:T(8,128)(2,1)}, u32[]{:S(2)}, u32[]{:S(2)}) collective-permute-start(bf16[3,2,384,128]{3,2,1,0:T(8,128)(2,1)S(1)} %pad_maximum_fusion.3.s0), channel_id=1, source_target_pairs={{0,16},{16,0},{32,48},{48,32},{64,80},{80,64},{96,112},{112,96},{1... | collective-permute-start | bytes 1769480 | tf_op jit(solution)/shard_map/ppermute | solution.py:32
  97.4 70.9 %collective-permute-start.14 = (bf16[6,2,384,128]{3,2,1,0:T(8,128)(2,1)S(1)}, bf16[6,2,384,128]{3,2,1,0:T(8,128)(2,1)S(1)}, u32[]{:S(2)}, u32[]{:S(2)}) collective-permute-start(bf16[6,2,384,128]{3,2,1,0:T(8,128)(2,1)S(1)} %pad_maximum_fusion.1.s0), channel_id=1, source_target_pairs={{0,16},{16,0},{32,48},{48,32},{64,80},{80,64},{96,112},{112,96},{1... | collective-permute-start | bytes 3538952 | tf_op jit(solution)/shard_map/ppermute | solution.py:32
  99.8 68.5 %collective-permute-start.15 = (bf16[6,2,384,128]{3,2,1,0:T(8,128)(2,1)S(1)}, bf16[6,2,384,128]{3,2,1,0:T(8,128)(2,1)S(1)}, u32[]{:S(2)}, u32[]{:S(2)}) collective-permute-start(bf16[6,2,384,128]{3,2,1,0:T(8,128)(2,1)S(1)} %pad_maximum_fusion.1.s0), channel_id=1, source_target_pairs={{16,32},{32,16},{48,64},{64,48},{80,96},{96,80},{17,33},{33,17},{4... | collective-permute-start | bytes 3538952 | tf_op jit(solution)/shard_map/ppermute | solution.py:32
  110.5 49.3 %collective-permute-start.25 = (bf16[3,2,384,128]{3,2,1,0:T(8,128)(2,1)S(1)}, bf16[3,2,384,128]{3,2,1,0:T(8,128)(2,1)S(1)}, u32[]{:S(2)}, u32[]{:S(2)}) collective-permute-start(bf16[3,2,384,128]{3,2,1,0:T(8,128)(2,1)S(1)} %pad_maximum_fusion.3.s0), channel_id=1, source_target_pairs={{16,32},{32,16},{48,64},{64,48},{80,96},{96,80},{17,33},{33,17},{4... | collective-permute-start | bytes 1769480 | tf_op jit(solution)/shard_map/ppermute | solution.py:32
  118.0 22.1 %collective-permute-start.17 = (f32[8,384]{1,0:T(8,128)S(1)}, f32[8,384]{1,0:T(8,128)S(1)}, u32[]{:S(2)}, u32[]{:S(2)}) collective-permute-start(f32[8,384]{1,0:T(8,128)S(1)} %get-tuple-element.19), channel_id=1, source_target_pairs={{128,256},{256,128},{129,257},{257,129},{130,258},{258,130},{131,2... | collective-permute-start | bytes 36872 | tf_op jit(solution)/shard_map/ppermute | solution.py:32
  118.6 23.9 %collective-permute-start.16 = (f32[8,384]{1,0:T(8,128)S(1)}, f32[8,384]{1,0:T(8,128)S(1)}, u32[]{:S(2)}, u32[]{:S(2)}) collective-permute-start(f32[8,384]{1,0:T(8,128)S(1)} %get-tuple-element.19), channel_id=1, source_target_pairs={{0,128},{128,0},{256,384},{384,256},{1,129},{129,1},{257,385},{385... | collective-permute-start | bytes 36872 | tf_op jit(solution)/shard_map/ppermute | solution.py:32
  155.3 9.1 %collective-permute-start.29 = (f32[3,8,384]{2,1,0:T(8,128)S(1)}, f32[3,8,384]{2,1,0:T(8,128)S(1)}, u32[]{:S(2)}, u32[]{:S(2)}) collective-permute-start(f32[3,8,384]{2,1,0:T(8,128)S(1)} %pad_maximum_fusion.9.r0), channel_id=1, source_target_pairs={{16,32},{32,16},{48,64},{64,48},{80,96},{96,80},{17,33},{33,17},{4... | collective-permute-start | bytes 110600 | tf_op jit(solution)/shard_map/ppermute | solution.py:32
  159.8 8.5 %collective-permute-start.20 = (f32[6,8,384]{2,1,0:T(8,128)S(1)}, f32[6,8,384]{2,1,0:T(8,128)S(1)}, u32[]{:S(2)}, u32[]{:S(2)}) collective-permute-start(f32[6,8,384]{2,1,0:T(8,128)S(1)} %pad_maximum_fusion.8.r0), channel_id=1, source_target_pairs={{0,16},{16,0},{32,48},{48,32},{64,80},{80,64},{96,112},{112,96},{1... | collective-permute-start | bytes 221192 | tf_op jit(solution)/shard_map/ppermute | solution.py:32
  (23 other events, 402.1 us)
where the time goes:
time: 173 us; the launch traced here: 171 us
  starting transfers between devices  105 us (61%)
  Pallas kernels  26.5 us (15%)
  waiting for transfers between devices  25.7 us (15%)
  local copies, waits for them, and re-layouts  6.59 us (4%)
  other arithmetic  6.24 us (4%)
    ppermute x30, starting transfers between devices, swap(): results.append(lax.ppermute(value, axis, pairs))  105 us
    pallas_call x5, Pallas kernels, run(): pl.pallas_call(kernel, out_shape=out_shape, in_specs=[smem if i < in_smem...  26.5 us
    ppermute x30, waiting for transfers between devices, swap(): results.append(lax.ppermute(value, axis, pairs))  25.7 us
    another operation x5, other arithmetic, halo_first(): first = jnp.stack([own] + swap(own, 'wa'))  3.8 us
  transfers between devices with their start and end apart: 30, of which 4 were waited for; matrix products, arithmetic and copies ran while one was open for 7% of the time, Pallas kernels for 14%

commit v1 on v0

v1 whole, which is shorter than its diff:
```python
import math

import jax
import jax.numpy as jnp
import numpy as np
from jax import lax
from jax.experimental import pallas as pl
from jax.experimental.pallas import tpu as pltpu
from jax.sharding import PartitionSpec as P

ROWS = 384
DEPTH = 128
SCALE = DEPTH ** -0.5
LOG2E = 1.4426950408889634
SCALE2 = SCALE * LOG2E
PLACES = 27
STAT_ROWS = 32
BLOCK_ROWS = 2 * ROWS + STAT_ROWS
LINE_ROWS = 2 * BLOCK_ROWS + STAT_ROWS
FORWARD_GROUP = 6
BACKWARD_GROUP = 3
MASKED = 1e30
VMEM_LIMIT = 40 * 1024 * 1024

OFFSETS = np.array(
    [[a - 1, b - 1, c - 1] for a in range(3) for b in range(3) for c in range(3)], dtype=np.int32
)
NT_DIMS = (((1,), (1,)), ((), ()))
NN_DIMS = (((1,), (0,)), ((), ()))


def swap(value, axis):
    size = lax.axis_size(axis)
    results = []
    for first in (0, 1):
        pairs = []
        for i in range(first, size - 1, 2):
            pairs += [(i, i + 1), (i + 1, i)]
        results.append(lax.ppermute(value, axis, pairs))
    return results


def allowed_slots(window_extent, pair_table):
    counts = window_extent.shape[:3]
    coords = (lax.axis_index("ta"), lax.axis_index("ha"), lax.axis_index("wa"))
    distance = jnp.abs(jnp.asarray(OFFSETS))
    inside = jnp.ones((27,), jnp.bool_)
    for axis in range(3):
        position = coords[axis] + jnp.asarray(OFFSETS[:, axis])
        inside = inside & (position >= 0) & (position < counts[axis])
    padded = jnp.pad(window_extent, ((1, 1), (1, 1), (1, 1), (0, 0)))
    near = lax.dynamic_slice(padded, coords + (jnp.int32(0),), (3, 3, 3, 3)).reshape(27, 3)
    kept = pair_table[0] == 1
    as_query = kept & inside & jnp.all(distance <= near[13][None, :], axis=1)
    as_key = kept[::-1] & inside & jnp.all(distance <= near, axis=1)
    both = jnp.stack([as_query, as_key]).astype(jnp.int32)
    place = jnp.zeros((3, 3, 3), jnp.int32)
    for axis, weight in ((0, 9), (1, 3), (2, 1)):
        sign = 1 - 2 * (coords[axis] % 2)
        shape = [1, 1, 1]
        shape[axis] = 3
        step = jnp.asarray(np.array([0, 1, -1], dtype=np.int32)) * sign + 1
        place = place + weight * step.reshape(shape)
    place = place.reshape(27)
    hot = place[:, None] == jnp.arange(27, dtype=jnp.int32)[None, :]
    slots = jnp.sum(jnp.where(hot[None], both[:, None, :], 0), axis=2)
    slots = slots.reshape(2, 3, 9)
    plane = slots[:, 0]
    rest = slots[:, 1:].transpose(0, 2, 1).reshape(2, 18)
    return jnp.concatenate([plane, rest], axis=1).reshape(2 * PLACES)


def matmul(left, right, dims):
    return lax.dot_general(left, right, dims, preferred_element_type=jnp.float32)


def thirds(wide):
    return [wide[:, i * DEPTH : (i + 1) * DEPTH] for i in range(ROWS // DEPTH)]


def compact(flags, near, rest, kv):
    place = jnp.int32(0)
    first = 0
    for part, count in [(x, 3) for x in near] + [(x, 6) for x in rest]:

        def body(i, place, first=first, part=part):
            flag = flags[first + i]

            @pl.when(flag == 1)
            def _():
                kv[place] = part[i, :2]

            return place + flag

        place = lax.fori_loop(0, count, body, place)
        first += count
    return place


def each_group(number, size, step):
    def body(group, carry):
        blocks, biases = [], []
        for k in range(size):
            at = group * size + k
            blocks.append(jnp.minimum(at, number - 1))
            biases.append(jnp.where(at < number, 0.0, MASKED).astype(jnp.float32))
        step(blocks, biases)
        return carry

    lax.fori_loop(0, lax.div(number + size - 1, size), body, 0)


def forward(
    flags, q_ref, g_ref, n0, n1, n2, s0, s1, s2,
    out_ref, stat_ref, norm_ref, delta_ref, kv, peak, total, acc, stat,
):
    number = compact(flags, (n0, n1, n2), (s0, s1, s2), kv)
    peak[...] = jnp.full(peak.shape, -MASKED, jnp.float32)
    total[...] = jnp.zeros(total.shape, jnp.float32)
    acc[...] = jnp.zeros(acc.shape, jnp.float32)

    def step(blocks, biases):
        query = q_ref[...]
        scores = [matmul(query, kv[b, 0], NT_DIMS) for b in blocks]
        old = peak[...]
        best = old
        for score, bias in zip(scores, biases):
            a, b, c = thirds(score)
            best = jnp.maximum(best, jnp.maximum(jnp.maximum(a, b), c) - bias)
        new = jnp.broadcast_to(jnp.max(best, axis=1, keepdims=True), best.shape)
        peak[...] = new
        shrink = jnp.exp2((old - new) * SCALE2)
        norm = new * SCALE2
        whole = total[...] * shrink
        mixed = acc[...] * shrink
        for block, score, bias in zip(blocks, scores, biases):
            at = norm + bias
            a, b, c = (jnp.exp2(x * SCALE2 - at) for x in thirds(score))
            whole = whole + (a + b + c)
            chance = jnp.concatenate([x.astype(jnp.bfloat16) for x in (a, b, c)], axis=1)
            mixed = mixed + matmul(chance, kv[block, 1], NN_DIMS)
        total[...] = whole
        acc[...] = mixed

    each_group(number, FORWARD_GROUP, step)
    whole = jnp.sum(total[...], axis=1, keepdims=True)
    mixed = acc[...] / whole
    out_ref[...] = mixed.astype(out_ref.dtype)
    delta = jnp.sum(mixed * g_ref[...].astype(jnp.float32), axis=1, keepdims=True)
    norm = peak[:, :1] * SCALE2 + jnp.log2(whole)
    lane = lax.broadcasted_iota(jnp.int32, (ROWS, DEPTH), 1)
    both = jnp.where(lane == 0, norm, delta).T[:8]
    stat[...] = jnp.zeros(stat.shape, jnp.float32)
    for kind in range(2):
        left = both[kind : kind + 1]
        for part in range(3):
            rounded = left.astype(jnp.bfloat16).astype(jnp.float32)
            left = left - rounded
            for c, piece in enumerate(thirds(rounded)):
                row = 9 * kind + 3 * part + c
                stat[row : row + 1] = piece
    stat_ref[...] = stat[...].astype(stat_ref.dtype)
    norm_ref[...] = jnp.broadcast_to(norm - math.log2(SCALE), norm_ref.shape)
    delta_ref[...] = jnp.broadcast_to(delta, delta_ref.shape)


def query_side(
    flags, q_ref, g_ref, norm_ref, delta_ref, n0, n1, n2, s0, s1, s2, out_ref, kv, acc
):
    number = compact(flags, (n0, n1, n2), (s0, s1, s2), kv)
    acc[...] = jnp.zeros(acc.shape, jnp.float32)

    def step(blocks, biases):
        query, grad = q_ref[...], g_ref[...]
        norm, delta = norm_ref[...], delta_ref[...]
        scores = [matmul(query, kv[b, 0], NT_DIMS) for b in blocks]
        grad_chances = [matmul(grad, kv[b, 1], NT_DIMS) for b in blocks]
        sum_of = acc[...]
        for block, score, grad_chance, bias in zip(blocks, scores, grad_chances, biases):
            at = norm + bias
            parts = [
                (jnp.exp2(x * SCALE2 - at) * (y - delta)).astype(jnp.bfloat16)
                for x, y in zip(thirds(score), thirds(grad_chance))
            ]
            sum_of = sum_of + matmul(jnp.concatenate(parts, axis=1), kv[block, 0], NN_DIMS)
        acc[...] = sum_of

    each_group(number, BACKWARD_GROUP, step)
    out_ref[...] = acc[...].astype(out_ref.dtype)


def key_side(
    flags, k_ref, v_ref, n0, n1, n2, m0, m1, m2,
    key_out, value_out, qg, rows, key_acc, value_acc,
):
    place = jnp.int32(0)
    slots = [(n, m, w, None) for n, m in zip((n0, n1, n2), (m0, m1, m2)) for w in range(3)]
    slots += [(None, m, w, t) for m in (m0, m1, m2) for w in range(3) for t in range(2)]
    for at, (near, rest, w, t) in enumerate(slots):
        flag = flags[PLACES + at]

        @pl.when(flag == 1)
        def _(place=place, near=near, rest=rest, w=w, t=t):
            if t is None:
                first = 2 * BLOCK_ROWS
                qg[place] = near[w, 2:]
            else:
                first = BLOCK_ROWS * t + 2 * ROWS
                qg[place, 0] = rest[w, first - 2 * ROWS : first - ROWS]
                qg[place, 1] = rest[w, first - ROWS : first]
            stat = rest[w, first : first + STAT_ROWS].astype(jnp.float32)
            for kind in range(2):
                for c in range(3):
                    high, mid, low = (stat[r : r + 1] for r in range(9 * kind + c, 9 * kind + c + 9, 3))
                    rows[place, kind : kind + 1, c * DEPTH : (c + 1) * DEPTH] = high + (mid + low)

        place = place + flag
    number = place
    key_acc[...] = jnp.zeros(key_acc.shape, jnp.float32)
    value_acc[...] = jnp.zeros(value_acc.shape, jnp.float32)

    def step(blocks, biases):
        key, value = k_ref[...], v_ref[...]
        scores = [matmul(key, qg[b, 0], NT_DIMS) for b in blocks]
        grad_chances = [matmul(value, qg[b, 1], NT_DIMS) for b in blocks]
        key_sum, value_sum = key_acc[...], value_acc[...]
        for block, score, grad_chance, bias in zip(blocks, scores, grad_chances, biases):
            stat = rows[block]
            chance = jnp.exp2(score * SCALE2 - (stat[0:1, :] + bias))
            grad_score = (chance * (grad_chance - stat[1:2, :])).astype(jnp.bfloat16)
            value_sum = value_sum + matmul(chance.astype(jnp.bfloat16), qg[block, 1], NN_DIMS)
            key_sum = key_sum + matmul(grad_score, qg[block, 0], NN_DIMS)
        key_acc[...] = key_sum
        value_acc[...] = value_sum

    each_group(number, BACKWARD_GROUP, step)
    key_out[...] = (key_acc[...] * SCALE).astype(key_out.dtype)
    value_out[...] = value_acc[...].astype(value_out.dtype)


def call(kernel, name, out_shape, scratch):
    smem = pl.BlockSpec(memory_space=pltpu.SMEM)
    vmem = pl.BlockSpec(memory_space=pltpu.VMEM)
    area = PLACES * ROWS * ROWS

    def run(*operands):
        return pl.pallas_call(
            kernel,
            out_shape=out_shape,
            in_specs=[smem] + [vmem] * (len(operands) - 1),
            out_specs=jax.tree.map(lambda _: vmem, out_shape),
            scratch_shapes=scratch,
            compiler_params=pltpu.CompilerParams(vmem_limit_bytes=VMEM_LIMIT),
            cost_estimate=pl.CostEstimate(
                flops=area * DEPTH * 8, transcendentals=area, bytes_accessed=PLACES * ROWS * DEPTH * 4
            ),
            name=name,
        )(*operands)

    return run


def join(parts, *after):
    count = len(parts)
    starts = np.cumsum([0] + [x.shape[0] for x in parts])

    def kernel(*refs):
        out = refs[-1]
        for i in range(count):
            out[int(starts[i]) : int(starts[i + 1])] = refs[i][...]

    vmem = pl.BlockSpec(memory_space=pltpu.VMEM)
    anywhere = pl.BlockSpec(memory_space=pl.ANY)
    return pl.pallas_call(
        kernel,
        out_shape=jax.ShapeDtypeStruct((int(starts[-1]),) + parts[0].shape[1:], parts[0].dtype),
        in_specs=[vmem] * count + [anywhere] * len(after),
        out_specs=vmem,
        compiler_params=pltpu.CompilerParams(vmem_limit_bytes=VMEM_LIMIT),
        name="join",
    )(*parts, *after)


def last_two(own, *after):
    def kernel(*refs):
        refs[-1][...] = refs[0][:, 2:]

    vmem = pl.BlockSpec(memory_space=pltpu.VMEM)
    anywhere = pl.BlockSpec(memory_space=pl.ANY)
    return pl.pallas_call(
        kernel,
        out_shape=jax.ShapeDtypeStruct((1, 2, ROWS, DEPTH), own.dtype),
        in_specs=[vmem] + [anywhere] * len(after),
        out_specs=vmem,
        compiler_params=pltpu.CompilerParams(vmem_limit_bytes=VMEM_LIMIT),
        name="last_two",
    )(own, *after)


def kernels():
    wide = jax.ShapeDtypeStruct((ROWS, DEPTH), jnp.float32)
    narrow = jax.ShapeDtypeStruct((ROWS, DEPTH), jnp.bfloat16)
    stat_shape = jax.ShapeDtypeStruct((STAT_ROWS, DEPTH), jnp.bfloat16)
    stat_scratch = pltpu.VMEM((STAT_ROWS, DEPTH), jnp.float32)
    blocks = pltpu.VMEM((PLACES, 2, ROWS, DEPTH), jnp.bfloat16)
    stats = pltpu.VMEM((PLACES, 8, ROWS), jnp.float32)
    wide_scratch = pltpu.VMEM((ROWS, DEPTH), jnp.float32)
    return (
        call(
            forward,
            "forward",
            (narrow, stat_shape, wide, wide),
            [blocks] + [wide_scratch] * 3 + [stat_scratch],
        ),
        call(query_side, "query_side", narrow, [blocks, wide_scratch]),
        call(key_side, "key_side", (narrow, narrow), [blocks, stats] + [wide_scratch] * 2),
    )


def on_device(queries, keys, values, out_grad, window_extent, pair_table):
    out_block = queries.shape
    q, k, v, g = (x.reshape(ROWS, DEPTH) for x in (queries, keys, values, out_grad))
    flags = allowed_slots(window_extent, pair_table)
    run_forward, run_query, run_key = kernels()

    kv = jnp.stack([k, v])[None]
    kv_planes = swap(kv, "ta")
    own = join([kv[0], q[None], g[None]])[None]
    near_row = join([own] + swap(own, "wa"))
    near = [near_row] + swap(near_row, "ha")
    kv_middle = join(kv_planes)
    kv_row = join([kv_middle] + swap(kv_middle, "wa"))
    kv_rest = [kv_row] + swap(kv_row, "ha")
    qg_planes = swap(last_two(own, kv_row), "ta")
    attended, stat, norm, delta = run_forward(flags, q, g, *near, *kv_rest)
    pieces = []
    for plane, plane_stat in zip(qg_planes, swap(stat, "ta")):
        pieces += [plane.reshape(2 * ROWS, DEPTH), plane_stat]
    line = join(pieces + [stat])[None]
    qg_row = join([line] + swap(line, "wa"))
    qg_rest = [qg_row] + swap(qg_row, "ha")
    query_grad = run_query(flags, q, g, norm, delta, *near, *kv_rest)
    key_grad, value_grad = run_key(flags, k, v, *near, *qg_rest)
    return tuple(x.reshape(out_block) for x in (attended, query_grad, key_grad, value_grad))


def solution(mesh):
    split = P("ta", "ha", "wa", None)
    return jax.shard_map(
        on_device,
        mesh=mesh,
        in_specs=(split, split, split, split, P(), P()),
        out_specs=(split, split, split, split),
        check_vma=False,
    )
```

time: 173 us -> 136 us (0.79)
  the two profiles are of different devices: /device:TPU:7 before, /device:TPU:143 now
where the time goes in v1:
time: 136 us
  starting transfers between devices  62.6 us (46%)
  waiting for transfers between devices  47.1 us (35%)
  Pallas kernels  18.4 us (14%)
  local copies, waits for them, and re-layouts  4.63 us (3%)
  other arithmetic  1.9 us (1%)
    ppermute x18, starting transfers between devices, swap(): results.append(lax.ppermute(value, axis, pairs))  62.6 us
    ppermute x18, waiting for transfers between devices, swap(): results.append(lax.ppermute(value, axis, pairs))  47.1 us
    pallas_call x3, Pallas kernels, run(): pl.pallas_call(kernel, out_shape=out_shape, in_specs=[smem] + [vmem] * (l...  18.1 us
    unnamed x30, local copies, waits for them, and re-layouts  3.61 us
  transfers between devices with their start and end apart: 18, of which 8 were waited for; matrix products, arithmetic and copies ran while one was open for 1% of the time, Pallas kernels for 7%

profile of v1, /device:TPU:143, one launch (start us, length us, event | category | flops | bytes accessed | tf_op | source)
XLA Modules:
  0.0 135.7 jit_solution(6595530581998816564)
XLA Ops:
  1.7 8.8 %collective-permute-start.5 = (bf16[1,2,384,128]{3,2,1,0:T(8,128)(2,1)S(1)}, bf16[1,2,384,128]{3,2,1,0:T(8,128)(2,1)S(1)}, u32[]{:S(2)}, u32[]{:S(2)}) collective-permute-start(bf16[1,2,384,128]{3,2,1,0:T(8,128)(2,1)S(1)} %get-tuple-element.20), channel_id=1, source_target_pairs={{128,256},{256,128},{129,257},{257,129},{130,258},{258,130},{131,2... | collective-permute-start | bytes 589832 | tf_op jit(solution)/shard_map/ppermute | solution.py:39
  10.5 1.9 %collective-permute-start.4 = (bf16[1,2,384,128]{3,2,1,0:T(8,128)(2,1)S(1)}, bf16[1,2,384,128]{3,2,1,0:T(8,128)(2,1)S(1)}, u32[]{:S(2)}, u32[]{:S(2)}) collective-permute-start(bf16[1,2,384,128]{3,2,1,0:T(8,128)(2,1)S(1)} %get-tuple-element.20), channel_id=1, source_target_pairs={{0,128},{128,0},{256,384},{384,256},{1,129},{129,1},{257,385},{385... | collective-permute-start | bytes 589832 | tf_op jit(solution)/shard_map/ppermute | solution.py:39
  14.2 2.6 %collective-permute-start.1 = (bf16[1,4,384,128]{3,2,1,0:T(8,128)(2,1)S(1)}, bf16[1,4,384,128]{3,2,1,0:T(8,128)(2,1)S(1)}, u32[]{:S(2)}, u32[]{:S(2)}) collective-permute-start(bf16[1,4,384,128]{3,2,1,0:T(8,128)(2,1)S(1)} %bitcast.31), channel_id=1, source_target_pairs={{1,2},{2,1},{3,4},{4,3},{5,6},{6,5},{7,8},{8,7},{9,10},{10,9},{11,... | collective-permute-start | bytes 1179656 | tf_op jit(solution)/shard_map/ppermute | solution.py:39
  16.8 2.1 %collective-permute-start = (bf16[1,4,384,128]{3,2,1,0:T(8,128)(2,1)S(1)}, bf16[1,4,384,128]{3,2,1,0:T(8,128)(2,1)S(1)}, u32[]{:S(2)}, u32[]{:S(2)}) collective-permute-start(bf16[1,4,384,128]{3,2,1,0:T(8,128)(2,1)S(1)} %bitcast.32), channel_id=1, source_target_pairs={{0,1},{1,0},{2,3},{3,2},{4,5},{5,4},{6,7},{7,6},{8,9},{9,8},{10,11... | collective-permute-start | bytes 1179656 | tf_op jit(solution)/shard_map/ppermute | solution.py:39
  19.0 9.1 %collective-permute-done.5.refs_1_ = bf16[1,2,384,128]{3,2,1,0:T(8,128)(2,1)S(1)} collective-permute-done((bf16[1,2,384,128]{3,2,1,0:T(8,128)(2,1)S(1)}, bf16[1,2,384,128]{3,2,1,0:T(8,128)(2,1)S(1)}, u32[]{:S(2)}, u32[]{:S(2)}) %collective-permute-start.5) | collective-permute-done | bytes 196640 | tf_op jit(solution)/shard_map/ppermute | solution.py:39
  28.2 1.9 %collective-permute-start.7 = (bf16[2,2,384,128]{3,2,1,0:T(8,128)(2,1)S(1)}, bf16[2,2,384,128]{3,2,1,0:T(8,128)(2,1)S(1)}, u32[]{:S(2)}, u32[]{:S(2)}) collective-permute-start(bf16[2,2,384,128]{3,2,1,0:T(8,128)(2,1)S(1)} %join.8.refs_0_), channel_id=1, source_target_pairs={{1,2},{2,1},{3,4},{4,3},{5,6},{6,5},{7,8},{8,7},{9,10},{10,9},{11,... | collective-permute-start | bytes 1179656 | tf_op jit(solution)/shard_map/ppermute | solution.py:39
  30.1 2.7 %collective-permute-start.6 = (bf16[2,2,384,128]{3,2,1,0:T(8,128)(2,1)S(1)}, bf16[2,2,384,128]{3,2,1,0:T(8,128)(2,1)S(1)}, u32[]{:S(2)}, u32[]{:S(2)}) collective-permute-start(bf16[2,2,384,128]{3,2,1,0:T(8,128)(2,1)S(1)} %join.8.refs_0_), channel_id=1, source_target_pairs={{0,1},{1,0},{2,3},{3,2},{4,5},{5,4},{6,7},{7,6},{8,9},{9,8},{10,11... | collective-permute-start | bytes 1179656 | tf_op jit(solution)/shard_map/ppermute | solution.py:39
  33.5 5.0 %collective-permute-done.1.refs_2_ = bf16[1,4,384,128]{3,2,1,0:T(8,128)(2,1)S(1)} collective-permute-done((bf16[1,4,384,128]{3,2,1,0:T(8,128)(2,1)S(1)}, bf16[1,4,384,128]{3,2,1,0:T(8,128)(2,1)S(1)}, u32[]{:S(2)}, u32[]{:S(2)}) %collective-permute-start.1) | collective-permute-done | bytes 393248 | tf_op jit(solution)/shard_map/ppermute | solution.py:39
  38.6 4.6 %collective-permute-start.3 = (bf16[3,4,384,128]{3,2,1,0:T(8,128)(2,1)S(1)}, bf16[3,4,384,128]{3,2,1,0:T(8,128)(2,1)}, u32[]{:S(2)}, u32[]{:S(2)}) collective-permute-start(bf16[3,4,384,128]{3,2,1,0:T(8,128)(2,1)S(1)} %join.7.n0), channel_id=1, source_target_pairs={{16,32},{32,16},{48,64},{64,48},{80,96},{96,80},{17,33},{33,17},{4... | collective-permute-start | bytes 3538952 | tf_op jit(solution)/shard_map/ppermute | solution.py:39
  43.2 1.9 %collective-permute-start.2 = (bf16[3,4,384,128]{3,2,1,0:T(8,128)(2,1)S(1)}, bf16[3,4,384,128]{3,2,1,0:T(8,128)(2,1)}, u32[]{:S(2)}, u32[]{:S(2)}) collective-permute-start(bf16[3,4,384,128]{3,2,1,0:T(8,128)(2,1)S(1)} %join.7.n0), channel_id=1, source_target_pairs={{0,16},{16,0},{32,48},{48,32},{64,80},{80,64},{96,112},{112,96},{1... | collective-permute-start | bytes 3538952 | tf_op jit(solution)/shard_map/ppermute | solution.py:39
  48.8 4.2 %collective-permute-start.9 = (bf16[6,2,384,128]{3,2,1,0:T(8,128)(2,1)S(1)}, bf16[6,2,384,128]{3,2,1,0:T(8,128)(2,1)}, u32[]{:S(2)}, u32[]{:S(2)}) collective-permute-start(bf16[6,2,384,128]{3,2,1,0:T(8,128)(2,1)S(1)} %join.9.s0.refs_1_), channel_id=1, source_target_pairs={{16,32},{32,16},{48,64},{64,48},{80,96},{96,80},{17,33},{33,17},{4... | collective-permute-start | bytes 3538952 | tf_op jit(solution)/shard_map/ppermute | solution.py:39
  53.0 1.9 %collective-permute-start.8 = (bf16[6,2,384,128]{3,2,1,0:T(8,128)(2,1)S(1)}, bf16[6,2,384,128]{3,2,1,0:T(8,128)(2,1)}, u32[]{:S(2)}, u32[]{:S(2)}) collective-permute-start(bf16[6,2,384,128]{3,2,1,0:T(8,128)(2,1)S(1)} %join.9.s0.refs_1_), channel_id=1, source_target_pairs={{0,16},{16,0},{32,48},{48,32},{64,80},{80,64},{96,112},{112,96},{1... | collective-permute-start | bytes 3538952 | tf_op jit(solution)/shard_map/ppermute | solution.py:39
  56.2 4.9 %collective-permute-start.12 = (bf16[1,2,384,128]{3,2,1,0:T(8,128)(2,1)S(1)}, bf16[1,2,384,128]{3,2,1,0:T(8,128)(2,1)S(1)}, u32[]{:S(2)}, u32[]{:S(2)}) collective-permute-start(bf16[1,2,384,128]{3,2,1,0:T(8,128)(2,1)S(1)} %last_two.1), channel_id=1, source_target_pairs={{128,256},{256,128},{129,257},{257,129},{130,258},{258,130},{131,2... | collective-permute-start | bytes 589832 | tf_op jit(solution)/shard_map/ppermute | solution.py:39
  63.0 7.0 %collective-permute-done.9.s2 = bf16[6,2,384,128]{3,2,1,0:T(8,128)(2,1)} collective-permute-done((bf16[6,2,384,128]{3,2,1,0:T(8,128)(2,1)S(1)}, bf16[6,2,384,128]{3,2,1,0:T(8,128)(2,1)}, u32[]{:S(2)}, u32[]{:S(2)}) %collective-permute-start.9) | collective-permute-done | bytes 1179680 | tf_op jit(solution)/shard_map/ppermute | solution.py:39
  70.0 5.2 %forward.1 = (bf16[384,128]{1,0:T(8,128)(2,1)}, bf16[32,128]{1,0:T(8,128)(2,1)S(1)}, f32[384,128]{1,0:T(8,128)S(1)}, f32[384,128]{1,0:T(8,128)S(1)}) custom-call(s32[54]{0:T(128)S(1)} %reshape.121.flags, bf16[384,128]{1,0:T(8,128)(2,1)S(1)} %bitcast.41, bf16[384,128]{1,0:T(8,128)(2,1)S(1)} %bitcast.44, bf16[3,4,384,128]{3,2,1,0:T(8,128)(2,1)S(1)} %join.7.n0, ...), custom_call_target="tpu_custom_call" | custom-call | flops 4076863488 | bytes 5308416 | tf_op jit(solution)/shard_map/forward/pallas_call | solution.py:247
  75.3 7.5 %collective-permute-start.13 = (bf16[32,128]{1,0:T(8,128)(2,1)S(1)}, bf16[32,128]{1,0:T(8,128)(2,1)S(1)}, u32[]{:S(2)}, u32[]{:S(2)}) collective-permute-start(bf16[32,128]{1,0:T(8,128)(2,1)S(1)} %get-tuple-element.13.refs_4_), channel_id=1, source_target_pairs={{128,256},{256,128},{129,257},{257,129},{130,258},{258,130},{131,2... | collective-permute-start | bytes 24584 | tf_op jit(solution)/shard_map/ppermute | solution.py:39
  84.8 6.4 %collective-permute-done.11.refs_1_ = bf16[32,128]{1,0:T(8,128)(2,1)S(1)} collective-permute-done((bf16[32,128]{1,0:T(8,128)(2,1)S(1)}, bf16[32,128]{1,0:T(8,128)(2,1)S(1)}, u32[]{:S(2)}, u32[]{:S(2)}) %collective-permute-start.11) | collective-permute-done | bytes 8224 | tf_op jit(solution)/shard_map/ppermute | solution.py:39
  91.2 2.7 %collective-permute-start.15 = (bf16[1,1632,128]{2,1,0:T(8,128)(2,1)S(1)}, bf16[1,1632,128]{2,1,0:T(8,128)(2,1)S(1)}, u32[]{:S(2)}, u32[]{:S(2)}) collective-permute-start(bf16[1,1632,128]{2,1,0:T(8,128)(2,1)S(1)} %bitcast.35), channel_id=1, source_target_pairs={{1,2},{2,1},{3,4},{4,3},{5,6},{6,5},{7,8},{8,7},{9,10},{10,9},{11,... | collective-permute-start | bytes 1253384 | tf_op jit(solution)/shard_map/ppermute | solution.py:39
  93.9 1.9 %collective-permute-start.14 = (bf16[1,1632,128]{2,1,0:T(8,128)(2,1)S(1)}, bf16[1,1632,128]{2,1,0:T(8,128)(2,1)S(1)}, u32[]{:S(2)}, u32[]{:S(2)}) collective-permute-start(bf16[1,1632,128]{2,1,0:T(8,128)(2,1)S(1)} %bitcast.36), channel_id=1, source_target_pairs={{0,1},{1,0},{2,3},{3,2},{4,5},{5,4},{6,7},{7,6},{8,9},{9,8},{10,11... | collective-permute-start | bytes 1253384 | tf_op jit(solution)/shard_map/ppermute | solution.py:39
  95.9 8.8 %collective-permute-done.15.refs_2_ = bf16[1,1632,128]{2,1,0:T(8,128)(2,1)S(1)} collective-permute-done((bf16[1,1632,128]{2,1,0:T(8,128)(2,1)S(1)}, bf16[1,1632,128]{2,1,0:T(8,128)(2,1)S(1)}, u32[]{:S(2)}, u32[]{:S(2)}) %collective-permute-start.15) | collective-permute-done | bytes 417824 | tf_op jit(solution)/shard_map/ppermute | solution.py:39
  105.4 7.2 %collective-permute-start.17 = (bf16[3,1632,128]{2,1,0:T(8,128)(2,1)S(1)}, bf16[3,1632,128]{2,1,0:T(8,128)(2,1)S(1)}, u32[]{:S(2)}, u32[]{:S(2)}) collective-permute-start(bf16[3,1632,128]{2,1,0:T(8,128)(2,1)S(1)} %join.11.m0), channel_id=1, source_target_pairs={{16,32},{32,16},{48,64},{64,48},{80,96},{96,80},{17,33},{33,17},{4... | collective-permute-start | bytes 3760136 | tf_op jit(solution)/shard_map/ppermute | solution.py:39
  114.6 4.4 %query_side.1 = bf16[384,128]{1,0:T(8,128)(2,1)} custom-call(s32[54]{0:T(128)S(1)} %reshape.121.flags, bf16[384,128]{1,0:T(8,128)(2,1)S(1)} %bitcast.42, bf16[384,128]{1,0:T(8,128)(2,1)S(1)} %bitcast.45, f32[384,128]{1,0:T(8,128)S(1)} %get-tuple-element.11.norm_ref, f32[384,128]{1,0:T(8,128)S(1)} %get-tuple-element.12.delta_ref, ...), custom_call_target="tpu_custom_call" | custom-call | flops 4076863488 | bytes 5308416 | tf_op jit(solution)/shard_map/query_side/pallas_call | solution.py:247
  119.0 8.3 %collective-permute-done.17.m2 = bf16[3,1632,128]{2,1,0:T(8,128)(2,1)S(1)} collective-permute-done((bf16[3,1632,128]{2,1,0:T(8,128)(2,1)S(1)}, bf16[3,1632,128]{2,1,0:T(8,128)(2,1)S(1)}, u32[]{:S(2)}, u32[]{:S(2)}) %collective-permute-start.17) | collective-permute-done | bytes 1253408 | tf_op jit(solution)/shard_map/ppermute | solution.py:39
  127.3 8.4 %key_side.1 = (bf16[384,128]{1,0:T(8,128)(2,1)}, bf16[384,128]{1,0:T(8,128)(2,1)}) custom-call(s32[54]{0:T(128)S(1)} %reshape.121.flags, bf16[384,128]{1,0:T(8,128)(2,1)S(1)} %bitcast.49, bf16[384,128]{1,0:T(8,128)(2,1)S(1)} %bitcast.47, bf16[3,4,384,128]{3,2,1,0:T(8,128)(2,1)S(1)} %join.7.n0, bf16[3,4,384,128]{3,2,1,0:T(8,128)(2,1)} %collective-permute-done.2.n1, ...), custom_call_target="tpu_custom_call" | custom-call | flops 4076863488 | bytes 5308416 | tf_op jit(solution)/shard_map/key_side/pallas_call | solution.py:247
  (76 shorter events, 15.1 us)
Async XLA Ops:
  0.6 18.3 %copy-start.14 = (s32[3]{0:T(128)S(1)}, s32[3]{0:T(128)}, u32[]{:S(2)}) copy-start(s32[3]{0:T(128)} %constant.72.clone) | copy-start | bytes 40
  0.6 32.2 %copy-start.10 = (s32[1,27]{1,0:T(1,128)S(1)}, s32[1,27]{1,0:T(1,128)}, u32[]{:S(2)}) copy-start(s32[1,27]{1,0:T(1,128)} %param.18) | copy-start | bytes 328
  0.7 32.4 %copy-start.8 = (s32[4,8,16,3]{2,1,3,0:T(8,128)S(1)}, s32[4,8,16,3]{2,1,3,0:T(8,128)}, u32[]{:S(2)}) copy-start(s32[4,8,16,3]{2,1,3,0:T(8,128)} %param.17) | copy-start | bytes 18436
  0.7 32.8 %copy-start.9 = (s32[27,3]{0,1:T(4,128)S(1)}, s32[27,3]{0,1:T(4,128)}, u32[]{:S(2)}) copy-start(s32[27,3]{0,1:T(4,128)} %constant.79) | copy-start | bytes 976
  1.7 26.5 %collective-permute-start.5 = (bf16[1,2,384,128]{3,2,1,0:T(8,128)(2,1)S(1)}, bf16[1,2,384,128]{3,2,1,0:T(8,128)(2,1)S(1)}, u32[]{:S(2)}, u32[]{:S(2)}) collective-permute-start(bf16[1,2,384,128]{3,2,1,0:T(8,128)(2,1)S(1)} %get-tuple-element.20), channel_id=1, source_target_pairs={{128,256},{256,128},{129,257},{257,129},{130,258},{258,130},{131,2... | collective-permute-start | bytes 589832 | tf_op jit(solution)/shard_map/ppermute | solution.py:39
  10.5 17.6 %collective-permute-start.4 = (bf16[1,2,384,128]{3,2,1,0:T(8,128)(2,1)S(1)}, bf16[1,2,384,128]{3,2,1,0:T(8,128)(2,1)S(1)}, u32[]{:S(2)}, u32[]{:S(2)}) collective-permute-start(bf16[1,2,384,128]{3,2,1,0:T(8,128)(2,1)S(1)} %get-tuple-element.20), channel_id=1, source_target_pairs={{0,128},{128,0},{256,384},{384,256},{1,129},{129,1},{257,385},{385... | collective-permute-start | bytes 589832 | tf_op jit(solution)/shard_map/ppermute | solution.py:39
  14.2 24.3 %collective-permute-start.1 = (bf16[1,4,384,128]{3,2,1,0:T(8,128)(2,1)S(1)}, bf16[1,4,384,128]{3,2,1,0:T(8,128)(2,1)S(1)}, u32[]{:S(2)}, u32[]{:S(2)}) collective-permute-start(bf16[1,4,384,128]{3,2,1,0:T(8,128)(2,1)S(1)} %bitcast.31), channel_id=1, source_target_pairs={{1,2},{2,1},{3,4},{4,3},{5,6},{6,5},{7,8},{8,7},{9,10},{10,9},{11,... | collective-permute-start | bytes 1179656 | tf_op jit(solution)/shard_map/ppermute | solution.py:39
  16.8 21.7 %collective-permute-start = (bf16[1,4,384,128]{3,2,1,0:T(8,128)(2,1)S(1)}, bf16[1,4,384,128]{3,2,1,0:T(8,128)(2,1)S(1)}, u32[]{:S(2)}, u32[]{:S(2)}) collective-permute-start(bf16[1,4,384,128]{3,2,1,0:T(8,128)(2,1)S(1)} %bitcast.32), channel_id=1, source_target_pairs={{0,1},{1,0},{2,3},{3,2},{4,5},{5,4},{6,7},{7,6},{8,9},{9,8},{10,11... | collective-permute-start | bytes 1179656 | tf_op jit(solution)/shard_map/ppermute | solution.py:39
  28.2 18.8 %collective-permute-start.7 = (bf16[2,2,384,128]{3,2,1,0:T(8,128)(2,1)S(1)}, bf16[2,2,384,128]{3,2,1,0:T(8,128)(2,1)S(1)}, u32[]{:S(2)}, u32[]{:S(2)}) collective-permute-start(bf16[2,2,384,128]{3,2,1,0:T(8,128)(2,1)S(1)} %join.8.refs_0_), channel_id=1, source_target_pairs={{1,2},{2,1},{3,4},{4,3},{5,6},{6,5},{7,8},{8,7},{9,10},{10,9},{11,... | collective-permute-start | bytes 1179656 | tf_op jit(solution)/shard_map/ppermute | solution.py:39
  30.1 16.8 %collective-permute-start.6 = (bf16[2,2,384,128]{3,2,1,0:T(8,128)(2,1)S(1)}, bf16[2,2,384,128]{3,2,1,0:T(8,128)(2,1)S(1)}, u32[]{:S(2)}, u32[]{:S(2)}) collective-permute-start(bf16[2,2,384,128]{3,2,1,0:T(8,128)(2,1)S(1)} %join.8.refs_0_), channel_id=1, source_target_pairs={{0,1},{1,0},{2,3},{3,2},{4,5},{5,4},{6,7},{7,6},{8,9},{9,8},{10,11... | collective-permute-start | bytes 1179656 | tf_op jit(solution)/shard_map/ppermute | solution.py:39
  38.6 22.5 %collective-permute-start.3 = (bf16[3,4,384,128]{3,2,1,0:T(8,128)(2,1)S(1)}, bf16[3,4,384,128]{3,2,1,0:T(8,128)(2,1)}, u32[]{:S(2)}, u32[]{:S(2)}) collective-permute-start(bf16[3,4,384,128]{3,2,1,0:T(8,128)(2,1)S(1)} %join.7.n0), channel_id=1, source_target_pairs={{16,32},{32,16},{48,64},{64,48},{80,96},{96,80},{17,33},{33,17},{4... | collective-permute-start | bytes 3538952 | tf_op jit(solution)/shard_map/ppermute | solution.py:39
  43.2 19.8 %collective-permute-start.2 = (bf16[3,4,384,128]{3,2,1,0:T(8,128)(2,1)S(1)}, bf16[3,4,384,128]{3,2,1,0:T(8,128)(2,1)}, u32[]{:S(2)}, u32[]{:S(2)}) collective-permute-start(bf16[3,4,384,128]{3,2,1,0:T(8,128)(2,1)S(1)} %join.7.n0), channel_id=1, source_target_pairs={{0,16},{16,0},{32,48},{48,32},{64,80},{80,64},{96,112},{112,96},{1... | collective-permute-start | bytes 3538952 | tf_op jit(solution)/shard_map/ppermute | solution.py:39
  48.8 21.3 %copy-start.3 = (bf16[6,8,8,128]{3,2,1,0:T(8,128)(2,1)S(1)}, bf16[6,8,8,128]{3,2,1,0:T(8,128)(2,1)}, u32[]{:S(2)}) copy-start(bf16[6,8,8,128]{3,2,1,0:T(8,128)(2,1)} %param.13) | copy-start | bytes 294916
  48.8 21.3 %copy-start.5 = (bf16[6,8,8,128]{3,2,1,0:T(8,128)(2,1)S(1)}, bf16[6,8,8,128]{3,2,1,0:T(8,128)(2,1)}, u32[]{:S(2)}) copy-start(bf16[6,8,8,128]{3,2,1,0:T(8,128)(2,1)} %param.16) | copy-start | bytes 294916
  48.8 21.2 %collective-permute-start.9 = (bf16[6,2,384,128]{3,2,1,0:T(8,128)(2,1)S(1)}, bf16[6,2,384,128]{3,2,1,0:T(8,128)(2,1)}, u32[]{:S(2)}, u32[]{:S(2)}) collective-permute-start(bf16[6,2,384,128]{3,2,1,0:T(8,128)(2,1)S(1)} %join.9.s0.refs_1_), channel_id=1, source_target_pairs={{16,32},{32,16},{48,64},{64,48},{80,96},{96,80},{17,33},{33,17},{4... | collective-permute-start | bytes 3538952 | tf_op jit(solution)/shard_map/ppermute | solution.py:39
  53.0 17.0 %collective-permute-start.8 = (bf16[6,2,384,128]{3,2,1,0:T(8,128)(2,1)S(1)}, bf16[6,2,384,128]{3,2,1,0:T(8,128)(2,1)}, u32[]{:S(2)}, u32[]{:S(2)}) collective-permute-start(bf16[6,2,384,128]{3,2,1,0:T(8,128)(2,1)S(1)} %join.9.s0.refs_1_), channel_id=1, source_target_pairs={{0,16},{16,0},{32,48},{48,32},{64,80},{80,64},{96,112},{112,96},{1... | collective-permute-start | bytes 3538952 | tf_op jit(solution)/shard_map/ppermute | solution.py:39
  56.2 28.5 %collective-permute-start.12 = (bf16[1,2,384,128]{3,2,1,0:T(8,128)(2,1)S(1)}, bf16[1,2,384,128]{3,2,1,0:T(8,128)(2,1)S(1)}, u32[]{:S(2)}, u32[]{:S(2)}) collective-permute-start(bf16[1,2,384,128]{3,2,1,0:T(8,128)(2,1)S(1)} %last_two.1), channel_id=1, source_target_pairs={{128,256},{256,128},{129,257},{257,129},{130,258},{258,130},{131,2... | collective-permute-start | bytes 589832 | tf_op jit(solution)/shard_map/ppermute | solution.py:39
  61.1 23.6 %collective-permute-start.10 = (bf16[1,2,384,128]{3,2,1,0:T(8,128)(2,1)S(1)}, bf16[1,2,384,128]{3,2,1,0:T(8,128)(2,1)S(1)}, u32[]{:S(2)}, u32[]{:S(2)}) collective-permute-start(bf16[1,2,384,128]{3,2,1,0:T(8,128)(2,1)S(1)} %last_two.1), channel_id=1, source_target_pairs={{0,128},{128,0},{256,384},{384,256},{1,129},{129,1},{257,385},{385... | collective-permute-start | bytes 589832 | tf_op jit(solution)/shard_map/ppermute | solution.py:39
  75.3 9.5 %collective-permute-start.13 = (bf16[32,128]{1,0:T(8,128)(2,1)S(1)}, bf16[32,128]{1,0:T(8,128)(2,1)S(1)}, u32[]{:S(2)}, u32[]{:S(2)}) collective-permute-start(bf16[32,128]{1,0:T(8,128)(2,1)S(1)} %get-tuple-element.13.refs_4_), channel_id=1, source_target_pairs={{128,256},{256,128},{129,257},{257,129},{130,258},{258,130},{131,2... | collective-permute-start | bytes 24584 | tf_op jit(solution)/shard_map/ppermute | solution.py:39
  82.8 8.4 %collective-permute-start.11 = (bf16[32,128]{1,0:T(8,128)(2,1)S(1)}, bf16[32,128]{1,0:T(8,128)(2,1)S(1)}, u32[]{:S(2)}, u32[]{:S(2)}) collective-permute-start(bf16[32,128]{1,0:T(8,128)(2,1)S(1)} %get-tuple-element.13.refs_4_), channel_id=1, source_target_pairs={{0,128},{128,0},{256,384},{384,256},{1,129},{129,1},{257,385},{385... | collective-permute-start | bytes 24584 | tf_op jit(solution)/shard_map/ppermute | solution.py:39
  91.2 13.4 %collective-permute-start.15 = (bf16[1,1632,128]{2,1,0:T(8,128)(2,1)S(1)}, bf16[1,1632,128]{2,1,0:T(8,128)(2,1)S(1)}, u32[]{:S(2)}, u32[]{:S(2)}) collective-permute-start(bf16[1,1632,128]{2,1,0:T(8,128)(2,1)S(1)} %bitcast.35), channel_id=1, source_target_pairs={{1,2},{2,1},{3,4},{4,3},{5,6},{6,5},{7,8},{8,7},{9,10},{10,9},{11,... | collective-permute-start | bytes 1253384 | tf_op jit(solution)/shard_map/ppermute | solution.py:39
  93.9 11.4 %collective-permute-start.14 = (bf16[1,1632,128]{2,1,0:T(8,128)(2,1)S(1)}, bf16[1,1632,128]{2,1,0:T(8,128)(2,1)S(1)}, u32[]{:S(2)}, u32[]{:S(2)}) collective-permute-start(bf16[1,1632,128]{2,1,0:T(8,128)(2,1)S(1)} %bitcast.36), channel_id=1, source_target_pairs={{0,1},{1,0},{2,3},{3,2},{4,5},{5,4},{6,7},{7,6},{8,9},{9,8},{10,11... | collective-permute-start | bytes 1253384 | tf_op jit(solution)/shard_map/ppermute | solution.py:39
  105.4 21.9 %collective-permute-start.17 = (bf16[3,1632,128]{2,1,0:T(8,128)(2,1)S(1)}, bf16[3,1632,128]{2,1,0:T(8,128)(2,1)S(1)}, u32[]{:S(2)}, u32[]{:S(2)}) collective-permute-start(bf16[3,1632,128]{2,1,0:T(8,128)(2,1)S(1)} %join.11.m0), channel_id=1, source_target_pairs={{16,32},{32,16},{48,64},{64,48},{80,96},{96,80},{17,33},{33,17},{4... | collective-permute-start | bytes 3760136 | tf_op jit(solution)/shard_map/ppermute | solution.py:39
  112.6 14.7 %collective-permute-start.16 = (bf16[3,1632,128]{2,1,0:T(8,128)(2,1)S(1)}, bf16[3,1632,128]{2,1,0:T(8,128)(2,1)S(1)}, u32[]{:S(2)}, u32[]{:S(2)}) collective-permute-start(bf16[3,1632,128]{2,1,0:T(8,128)(2,1)S(1)} %join.11.m0), channel_id=1, source_target_pairs={{0,16},{16,0},{32,48},{48,32},{64,80},{80,64},{96,112},{112,96},{1... | collective-permute-start | bytes 3760136 | tf_op jit(solution)/shard_map/ppermute | solution.py:39
  (9 other events, 78.3 us)

commit v2 on v1

v2 whole, which is shorter than its diff:
```python
import math

import jax
import jax.numpy as jnp
import numpy as np
from jax import lax
from jax.experimental import pallas as pl
from jax.experimental.pallas import tpu as pltpu
from jax.sharding import PartitionSpec as P

ROWS = 384
DEPTH = 128
SCALE = DEPTH ** -0.5
LOG2E = 1.4426950408889634
SCALE2 = SCALE * LOG2E
PLACES = 27
STAT_ROWS = 32
BLOCK_ROWS = 2 * ROWS + STAT_ROWS
LINE_ROWS = 2 * BLOCK_ROWS + STAT_ROWS
NEAR_GROUP = 4
REST_GROUP = 5
BACKWARD_GROUP = 3
MASKED = 1e30
VMEM_LIMIT = 24 * 1024 * 1024
JOIN_LIMIT = 8 * 1024 * 1024

OFFSETS = np.array(
    [[a - 1, b - 1, c - 1] for a in range(3) for b in range(3) for c in range(3)], dtype=np.int32
)
NT_DIMS = (((1,), (1,)), ((), ()))
NN_DIMS = (((1,), (0,)), ((), ()))


def swap(value, axis):
    size = lax.axis_size(axis)
    results = []
    for first in (0, 1):
        pairs = []
        for i in range(first, size - 1, 2):
            pairs += [(i, i + 1), (i + 1, i)]
        results.append(lax.ppermute(value, axis, pairs))
    return results


def allowed_slots(window_extent, pair_table):
    counts = window_extent.shape[:3]
    coords = (lax.axis_index("ta"), lax.axis_index("ha"), lax.axis_index("wa"))
    distance = jnp.abs(jnp.asarray(OFFSETS))
    inside = jnp.ones((27,), jnp.bool_)
    for axis in range(3):
        position = coords[axis] + jnp.asarray(OFFSETS[:, axis])
        inside = inside & (position >= 0) & (position < counts[axis])
    padded = jnp.pad(window_extent, ((1, 1), (1, 1), (1, 1), (0, 0)))
    near = lax.dynamic_slice(padded, coords + (jnp.int32(0),), (3, 3, 3, 3)).reshape(27, 3)
    kept = pair_table[0] == 1
    as_query = kept & inside & jnp.all(distance <= near[13][None, :], axis=1)
    as_key = kept[::-1] & inside & jnp.all(distance <= near, axis=1)
    both = jnp.stack([as_query, as_key]).astype(jnp.int32)
    place = jnp.zeros((3, 3, 3), jnp.int32)
    for axis, weight in ((0, 9), (1, 3), (2, 1)):
        sign = 1 - 2 * (coords[axis] % 2)
        shape = [1, 1, 1]
        shape[axis] = 3
        step = jnp.asarray(np.array([0, 1, -1], dtype=np.int32)) * sign + 1
        place = place + weight * step.reshape(shape)
    place = place.reshape(27)
    hot = place[:, None] == jnp.arange(27, dtype=jnp.int32)[None, :]
    slots = jnp.sum(jnp.where(hot[None], both[:, None, :], 0), axis=2)
    query_slots = slots[0].reshape(3, 9)
    return jnp.concatenate(
        [
            query_slots[0],
            query_slots[1:].T.reshape(18),
            slots[1].reshape(3, 9).T.reshape(PLACES),
        ]
    )


def matmul(left, right, dims):
    return lax.dot_general(left, right, dims, preferred_element_type=jnp.float32)


def thirds(wide):
    return [wide[:, i * DEPTH : (i + 1) * DEPTH] for i in range(ROWS // DEPTH)]


def each_flag(flags, first, count, place, act):
    def body(i, place):
        flag = flags[first + i]

        @pl.when(flag == 1)
        def _():
            act(i, place)

        return place + flag

    return lax.fori_loop(0, count, body, place)


def collect(flags, held, remote, kv, sems):
    data = pl.ds(0, 2 * ROWS)
    ready = jnp.int32(0)
    for _, first, count in held:
        for i in range(count):
            ready = ready + flags[first + i]
    number = ready
    for part, first, count in remote:

        def start(i, place, part=part):
            pltpu.make_async_copy(part.at[i, data], kv.at[place], sems.at[place]).start()

        number = each_flag(flags, first, count, number, start)
    place = jnp.int32(0)
    for part, first, count in held:

        def move(i, place, part=part):
            kv[place] = part[i, : 2 * ROWS]

        place = each_flag(flags, first, count, place, move)

    def wait(at):
        @pl.when(at >= ready)
        def _():
            pltpu.make_async_copy(kv.at[at], kv.at[at], sems.at[at]).wait()

    return number, wait


def no_wait(at):
    del at


def each_group(number, size, wait, step):
    def body(group, carry):
        blocks, biases = [], []
        for k in range(size):
            at = group * size + k

            @pl.when(at < number)
            def _(at=at):
                wait(at)

            blocks.append(jnp.minimum(at, number - 1))
            biases.append(jnp.where(at < number, 0.0, MASKED).astype(jnp.float32))
        step(blocks, biases)
        return carry

    lax.fori_loop(0, lax.div(number + size - 1, size), body, 0)


def forward_groups(number, size, wait, q_ref, kv, peak, total, acc):
    def step(blocks, biases):
        query = q_ref[...]
        scores = [matmul(query, kv[b, :ROWS], NT_DIMS) for b in blocks]
        old = peak[...]
        best = old
        for score, bias in zip(scores, biases):
            a, b, c = thirds(score)
            best = jnp.maximum(best, jnp.maximum(jnp.maximum(a, b), c) - bias)
        new = jnp.broadcast_to(jnp.max(best, axis=1, keepdims=True), best.shape)
        peak[...] = new
        shrink = jnp.exp2((old - new) * SCALE2)
        norm = new * SCALE2
        whole = total[...] * shrink
        mixed = acc[...] * shrink
        for block, score, bias in zip(blocks, scores, biases):
            at = norm + bias
            a, b, c = (jnp.exp2(x * SCALE2 - at) for x in thirds(score))
            whole = whole + (a + b + c)
            chance = jnp.concatenate([x.astype(jnp.bfloat16) for x in (a, b, c)], axis=1)
            mixed = mixed + matmul(chance, kv[block, ROWS:], NN_DIMS)
        total[...] = whole
        acc[...] = mixed

    each_group(number, size, wait, step)


def forward_near(flags, q_ref, n0, n1, n2, peak, total, acc, kv, sems):
    number, wait = collect(flags, [(n0, 0, 3)], [(n1, 3, 3), (n2, 6, 3)], kv, sems)
    peak[...] = jnp.full(peak.shape, -MASKED, jnp.float32)
    total[...] = jnp.zeros(total.shape, jnp.float32)
    acc[...] = jnp.zeros(acc.shape, jnp.float32)
    forward_groups(number, NEAR_GROUP, wait, q_ref, kv, peak, total, acc)


def forward_rest(
    flags, q_ref, g_ref, s0, s1, s2, peak_in, total_in, acc_in,
    out_ref, stat_ref, norm_ref, delta_ref, kv, sems, peak, total, acc, stat,
):
    number, wait = collect(flags, [(s0, 9, 6)], [(s1, 15, 6), (s2, 21, 6)], kv, sems)
    peak[...] = peak_in[...]
    total[...] = total_in[...]
    acc[...] = acc_in[...]
    forward_groups(number, REST_GROUP, wait, q_ref, kv, peak, total, acc)
    whole = jnp.sum(total[...], axis=1, keepdims=True)
    mixed = acc[...] / whole
    out_ref[...] = mixed.astype(out_ref.dtype)
    delta = jnp.sum(mixed * g_ref[...].astype(jnp.float32), axis=1, keepdims=True)
    norm = peak[:, :1] * SCALE2 + jnp.log2(whole)
    lane = lax.broadcasted_iota(jnp.int32, (ROWS, DEPTH), 1)
    both = jnp.where(lane == 0, norm, delta).T[:8]
    stat[...] = jnp.zeros(stat.shape, jnp.float32)
    for kind in range(2):
        left = both[kind : kind + 1]
        for part in range(3):
            rounded = left.astype(jnp.bfloat16).astype(jnp.float32)
            left = left - rounded
            for c, piece in enumerate(thirds(rounded)):
                row = 9 * kind + 3 * part + c
                stat[row : row + 1] = piece
    stat_ref[...] = stat[...].astype(stat_ref.dtype)
    norm_ref[...] = jnp.broadcast_to(norm - math.log2(SCALE), norm_ref.shape)
    delta_ref[...] = jnp.broadcast_to(delta, delta_ref.shape)


def query_side(
    flags, q_ref, g_ref, norm_ref, delta_ref, n0, s0, n1, n2, s1, s2, out_ref, kv, sems, acc
):
    held = [(n0, 0, 3), (s0, 9, 6)]
    remote = [(n1, 3, 3), (n2, 6, 3), (s1, 15, 6), (s2, 21, 6)]
    number, wait = collect(flags, held, remote, kv, sems)
    acc[...] = jnp.zeros(acc.shape, jnp.float32)

    def step(blocks, biases):
        query, grad = q_ref[...], g_ref[...]
        norm, delta = norm_ref[...], delta_ref[...]
        scores = [matmul(query, kv[b, :ROWS], NT_DIMS) for b in blocks]
        grad_chances = [matmul(grad, kv[b, ROWS:], NT_DIMS) for b in blocks]
        sum_of = acc[...]
        for block, score, grad_chance, bias in zip(blocks, scores, grad_chances, biases):
            at = norm + bias
            parts = [
                (jnp.exp2(x * SCALE2 - at) * (y - delta)).astype(jnp.bfloat16)
                for x, y in zip(thirds(score), thirds(grad_chance))
            ]
            sum_of = sum_of + matmul(jnp.concatenate(parts, axis=1), kv[block, :ROWS], NN_DIMS)
        acc[...] = sum_of

    each_group(number, BACKWARD_GROUP, wait, step)
    out_ref[...] = acc[...].astype(out_ref.dtype)


def stat_rows(stat):
    for kind in range(2):
        pieces = []
        for row in range(9 * kind, 9 * kind + 3):
            pieces.append(stat[row : row + 1] + (stat[row + 3 : row + 4] + stat[row + 6 : row + 7]))
        yield jnp.concatenate(pieces, axis=1)


def key_side(
    flags, k_ref, v_ref, n0, l0, l1, l2, m0, m1, m2, n1, n2, key_out, value_out, qg, sems, key_acc, value_acc
):
    slots = []
    for near, line, columns in ((n0, l0, m0), (n1, l1, m1), (n2, l2, m2)):
        for w, rows in enumerate((line, columns.at[0], columns.at[1])):
            slots += [(near, w, rows, t) for t in range(3)]
    data = pl.ds(0, 2 * ROWS)

    def each_slot(act):
        place = jnp.int32(0)
        for at, (near, w, rows, t) in enumerate(slots):
            flag = flags[PLACES + at]
            pl.when(flag == 1)(lambda place=place, slot=(near, w, rows, t): act(place, *slot))
            place = place + flag
        return place

    def start(place, near, w, rows, t):
        if t == 0 and near is not n0:
            source = near.at[w, pl.ds(2 * ROWS, 2 * ROWS)]
            pltpu.make_async_copy(source, qg.at[place, data], sems.at[place]).start()

    def move(place, near, w, rows, t):
        if t > 0:
            qg[place] = rows[BLOCK_ROWS * (t - 1) : BLOCK_ROWS * t]
        else:
            qg[place, 2 * ROWS :] = rows[2 * BLOCK_ROWS :]
            if near is n0:
                qg[place, : 2 * ROWS] = near[w, 2 * ROWS :]

    def wait(place, near, w, rows, t):
        if t == 0 and near is not n0:
            pltpu.make_async_copy(qg.at[place, data], qg.at[place, data], sems.at[place]).wait()

    each_slot(start)
    number = each_slot(move)
    each_slot(wait)
    key_acc[...] = jnp.zeros(key_acc.shape, jnp.float32)
    value_acc[...] = jnp.zeros(value_acc.shape, jnp.float32)

    def step(blocks, biases):
        key, value = k_ref[...], v_ref[...]
        scores = [matmul(key, qg[b, :ROWS], NT_DIMS) for b in blocks]
        grad_chances = [matmul(value, qg[b, ROWS : 2 * ROWS], NT_DIMS) for b in blocks]
        key_sum, value_sum = key_acc[...], value_acc[...]
        for block, score, grad_chance, bias in zip(blocks, scores, grad_chances, biases):
            norm, delta = stat_rows(qg[block, 2 * ROWS :].astype(jnp.float32))
            chance = jnp.exp2(score * SCALE2 - (norm + bias))
            grad_score = (chance * (grad_chance - delta)).astype(jnp.bfloat16)
            value_sum = value_sum + matmul(chance.astype(jnp.bfloat16), qg[block, ROWS : 2 * ROWS], NN_DIMS)
            key_sum = key_sum + matmul(grad_score, qg[block, :ROWS], NN_DIMS)
        key_acc[...] = key_sum
        value_acc[...] = value_sum

    each_group(number, BACKWARD_GROUP, no_wait, step)
    key_out[...] = (key_acc[...] * SCALE).astype(key_out.dtype)
    value_out[...] = value_acc[...].astype(value_out.dtype)


def call(kernel, name, halo, out_shape, scratch):
    smem = pl.BlockSpec(memory_space=pltpu.SMEM)
    vmem = pl.BlockSpec(memory_space=pltpu.VMEM)
    anywhere = pl.BlockSpec(memory_space=pl.ANY)
    area = PLACES * ROWS * ROWS

    def run(*operands):
        return pl.pallas_call(
            kernel,
            out_shape=out_shape,
            in_specs=[smem]
            + [anywhere if i in halo else vmem for i in range(1, len(operands))],
            out_specs=jax.tree.map(lambda _: vmem, out_shape),
            scratch_shapes=scratch,
            compiler_params=pltpu.CompilerParams(vmem_limit_bytes=VMEM_LIMIT),
            cost_estimate=pl.CostEstimate(
                flops=area * DEPTH * 8, transcendentals=area, bytes_accessed=PLACES * ROWS * DEPTH * 4
            ),
            name=name,
        )(*operands)

    return run


def join(parts, *after):
    count = len(parts)
    starts = np.cumsum([0] + [x.shape[0] for x in parts])

    def kernel(*refs):
        out = refs[-1]
        for i in range(count):
            out[int(starts[i]) : int(starts[i + 1])] = refs[i][...]

    vmem = pl.BlockSpec(memory_space=pltpu.VMEM)
    anywhere = pl.BlockSpec(memory_space=pl.ANY)
    return pl.pallas_call(
        kernel,
        out_shape=jax.ShapeDtypeStruct((int(starts[-1]),) + parts[0].shape[1:], parts[0].dtype),
        in_specs=[vmem] * count + [anywhere] * len(after),
        out_specs=vmem,
        compiler_params=pltpu.CompilerParams(vmem_limit_bytes=JOIN_LIMIT),
        name="join",
    )(*parts, *after)


def last_two(own, *after):
    def kernel(*refs):
        refs[-1][...] = refs[0][:, 2:]

    vmem = pl.BlockSpec(memory_space=pltpu.VMEM)
    anywhere = pl.BlockSpec(memory_space=pl.ANY)
    return pl.pallas_call(
        kernel,
        out_shape=jax.ShapeDtypeStruct((1, 2, ROWS, DEPTH), own.dtype),
        in_specs=[vmem] + [anywhere] * len(after),
        out_specs=vmem,
        compiler_params=pltpu.CompilerParams(vmem_limit_bytes=JOIN_LIMIT),
        name="last_two",
    )(own, *after)


def kernels():
    wide = jax.ShapeDtypeStruct((ROWS, DEPTH), jnp.float32)
    narrow = jax.ShapeDtypeStruct((ROWS, DEPTH), jnp.bfloat16)
    stat_shape = jax.ShapeDtypeStruct((STAT_ROWS, DEPTH), jnp.bfloat16)
    stat_scratch = pltpu.VMEM((STAT_ROWS, DEPTH), jnp.float32)
    blocks = pltpu.VMEM((PLACES, 2 * ROWS, DEPTH), jnp.bfloat16)
    stat_blocks = pltpu.VMEM((PLACES, BLOCK_ROWS, DEPTH), jnp.bfloat16)
    sems = pltpu.SemaphoreType.DMA((PLACES,))
    wide_scratch = pltpu.VMEM((ROWS, DEPTH), jnp.float32)
    return (
        call(forward_near, "forward_near", range(3, 5), (wide, wide, wide), [blocks, sems]),
        call(
            forward_rest,
            "forward_rest",
            range(4, 6),
            (narrow, stat_shape, wide, wide),
            [blocks, sems] + [wide_scratch] * 3 + [stat_scratch],
        ),
        call(query_side, "query_side", range(7, 11), narrow, [blocks, sems, wide_scratch]),
        call(
            key_side,
            "key_side",
            range(10, 12),
            (narrow, narrow),
            [stat_blocks, sems] + [wide_scratch] * 2,
        ),
    )


def on_device(queries, keys, values, out_grad, window_extent, pair_table):
    out_block = queries.shape
    q, k, v, g = (x.reshape(ROWS, DEPTH) for x in (queries, keys, values, out_grad))
    flags = allowed_slots(window_extent, pair_table)
    run_near, run_rest, run_query, run_key = kernels()

    kv = jnp.stack([k, v])[None]
    kv_planes = swap(kv, "ta")
    own = join([kv[0], q[None], g[None]])[None]
    near_row = join([own] + swap(own, "wa"))
    near = [x.reshape(3, 4 * ROWS, DEPTH) for x in [near_row] + swap(near_row, "ha")]
    kv_middle = join(kv_planes)
    kv_row = join([kv_middle] + swap(kv_middle, "wa"))
    kv_rest = [x.reshape(6, 2 * ROWS, DEPTH) for x in [kv_row] + swap(kv_row, "ha")]
    qg_planes = swap(last_two(own, kv_row), "ta")
    state = run_near(flags, q, *near)
    attended, stat, norm, delta = run_rest(flags, q, g, *kv_rest, *state)
    pieces = []
    for plane, plane_stat in zip(qg_planes, swap(stat, "ta")):
        pieces += [plane.reshape(2 * ROWS, DEPTH), plane_stat]
    line = join(pieces + [stat])
    sides = swap(line, "wa")
    lines = [line] + swap(line, "ha")
    columns = join([x[None] for x in sides], *lines[1:])
    columns = [columns] + swap(columns, "ha")
    query_grad = run_query(
        flags, q, g, norm, delta, near[0], kv_rest[0], *near[1:], *kv_rest[1:]
    )
    key_grad, value_grad = run_key(flags, k, v, near[0], *lines, *columns, *near[1:])
    return tuple(x.reshape(out_block) for x in (attended, query_grad, key_grad, value_grad))


def solution(mesh):
    split = P("ta", "ha", "wa", None)
    return jax.shard_map(
        on_device,
        mesh=mesh,
        in_specs=(split, split, split, split, P(), P()),
        out_specs=(split, split, split, split),
        check_vma=False,
    )
```

time: 136 us -> 131 us (0.963)
  the two profiles are of different devices: /device:TPU:143 before, /device:TPU:7 now
where the time goes in v2:
time: 131 us; the launch traced here: 128 us
  starting transfers between devices  81.8 us (62%)
  Pallas kernels  22.9 us (17%)
  waiting for transfers between devices  17.2 us (13%)
  local copies, waits for them, and re-layouts  3.35 us (3%)
  other arithmetic  1.92 us (1%)
    ppermute x20, starting transfers between devices, swap(): results.append(lax.ppermute(value, axis, pairs))  81.8 us
    pallas_call x4, Pallas kernels, run(): pl.pallas_call(kernel, out_shape=out_shape, in_specs=[smem] + [anywhere i...  22.6 us
    ppermute x20, waiting for transfers between devices, swap(): results.append(lax.ppermute(value, axis, pairs))  17.2 us
  transfers between devices with their start and end apart: 20, of which 8 were waited for; matrix products, arithmetic and copies ran while one was open for 2% of the time, Pallas kernels for 12%

profile of v2, /device:TPU:7, one launch (start us, length us, event | category | flops | bytes accessed | tf_op | source)
XLA Modules:
  0.0 128.3 jit_solution(10140848474095679862)
XLA Ops:
  2.4 17.0 %collective-permute-start = (bf16[1,2,384,128]{3,2,1,0:T(8,128)(2,1)S(1)}, bf16[1,2,384,128]{3,2,1,0:T(8,128)(2,1)S(1)}, u32[]{:S(2)}, u32[]{:S(2)}) collective-permute-start(bf16[1,2,384,128]{3,2,1,0:T(8,128)(2,1)S(1)} %get-tuple-element.27), channel_id=1, source_target_pairs={{0,128},{128,0},{256,384},{384,256},{1,129},{129,1},{257,385},{385... | collective-permute-start | bytes 589832 | tf_op jit(solution)/shard_map/ppermute | solution.py:41
  21.2 2.6 %collective-permute-start.7 = (bf16[1,4,384,128]{3,2,1,0:T(8,128)(2,1)S(1)}, bf16[1,4,384,128]{3,2,1,0:T(8,128)(2,1)S(1)}, u32[]{:S(2)}, u32[]{:S(2)}) collective-permute-start(bf16[1,4,384,128]{3,2,1,0:T(8,128)(2,1)S(1)} %bitcast.39), channel_id=1, source_target_pairs={{1,2},{2,1},{3,4},{4,3},{5,6},{6,5},{7,8},{8,7},{9,10},{10,9},{11,... | collective-permute-start | bytes 1179656 | tf_op jit(solution)/shard_map/ppermute | solution.py:41
  23.7 2.1 %collective-permute-start.6 = (bf16[1,4,384,128]{3,2,1,0:T(8,128)(2,1)S(1)}, bf16[1,4,384,128]{3,2,1,0:T(8,128)(2,1)S(1)}, u32[]{:S(2)}, u32[]{:S(2)}) collective-permute-start(bf16[1,4,384,128]{3,2,1,0:T(8,128)(2,1)S(1)} %bitcast.40), channel_id=1, source_target_pairs={{0,1},{1,0},{2,3},{3,2},{4,5},{5,4},{6,7},{7,6},{8,9},{9,8},{10,11... | collective-permute-start | bytes 1179656 | tf_op jit(solution)/shard_map/ppermute | solution.py:41
  26.5 8.6 %collective-permute-done.refs_0_ = bf16[1,2,384,128]{3,2,1,0:T(8,128)(2,1)S(1)} collective-permute-done((bf16[1,2,384,128]{3,2,1,0:T(8,128)(2,1)S(1)}, bf16[1,2,384,128]{3,2,1,0:T(8,128)(2,1)S(1)}, u32[]{:S(2)}, u32[]{:S(2)}) %collective-permute-start) | collective-permute-done | bytes 196640 | tf_op jit(solution)/shard_map/ppermute | solution.py:41
  35.1 1.9 %collective-permute-start.3 = (bf16[2,2,384,128]{3,2,1,0:T(8,128)(2,1)S(1)}, bf16[2,2,384,128]{3,2,1,0:T(8,128)(2,1)S(1)}, u32[]{:S(2)}, u32[]{:S(2)}) collective-permute-start(bf16[2,2,384,128]{3,2,1,0:T(8,128)(2,1)S(1)} %join.6.refs_0_), channel_id=1, source_target_pairs={{1,2},{2,1},{3,4},{4,3},{5,6},{6,5},{7,8},{8,7},{9,10},{10,9},{11,... | collective-permute-start | bytes 1179656 | tf_op jit(solution)/shard_map/ppermute | solution.py:41
  37.0 2.7 %collective-permute-start.2 = (bf16[2,2,384,128]{3,2,1,0:T(8,128)(2,1)S(1)}, bf16[2,2,384,128]{3,2,1,0:T(8,128)(2,1)S(1)}, u32[]{:S(2)}, u32[]{:S(2)}) collective-permute-start(bf16[2,2,384,128]{3,2,1,0:T(8,128)(2,1)S(1)} %join.6.refs_0_), channel_id=1, source_target_pairs={{0,1},{1,0},{2,3},{3,2},{4,5},{5,4},{6,7},{7,6},{8,9},{9,8},{10,11... | collective-permute-start | bytes 1179656 | tf_op jit(solution)/shard_map/ppermute | solution.py:41
  39.9 6.1 %collective-permute-start.9 = (bf16[3,4,384,128]{3,2,1,0:T(8,128)(2,1)S(1)}, bf16[3,4,384,128]{3,2,1,0:T(8,128)(2,1)}, u32[]{:S(2)}, u32[]{:S(2)}) collective-permute-start(bf16[3,4,384,128]{3,2,1,0:T(8,128)(2,1)S(1)} %join.9), channel_id=1, source_target_pairs={{16,32},{32,16},{48,64},{64,48},{80,96},{96,80},{17,33},{33,17},{4... | collective-permute-start | bytes 3538952 | tf_op jit(solution)/shard_map/ppermute | solution.py:41
  45.9 1.9 %collective-permute-start.8 = (bf16[3,4,384,128]{3,2,1,0:T(8,128)(2,1)S(1)}, bf16[3,4,384,128]{3,2,1,0:T(8,128)(2,1)}, u32[]{:S(2)}, u32[]{:S(2)}) collective-permute-start(bf16[3,4,384,128]{3,2,1,0:T(8,128)(2,1)S(1)} %join.9), channel_id=1, source_target_pairs={{0,16},{16,0},{32,48},{48,32},{64,80},{80,64},{96,112},{112,96},{1... | collective-permute-start | bytes 3538952 | tf_op jit(solution)/shard_map/ppermute | solution.py:41
  48.9 5.1 %collective-permute-start.5 = (bf16[6,2,384,128]{3,2,1,0:T(8,128)(2,1)S(1)}, bf16[6,2,384,128]{3,2,1,0:T(8,128)(2,1)}, u32[]{:S(2)}, u32[]{:S(2)}) collective-permute-start(bf16[6,2,384,128]{3,2,1,0:T(8,128)(2,1)S(1)} %join.7.refs_1_), channel_id=1, source_target_pairs={{16,32},{32,16},{48,64},{64,48},{80,96},{96,80},{17,33},{33,17},{4... | collective-permute-start | bytes 3538952 | tf_op jit(solution)/shard_map/ppermute | solution.py:41
  54.0 1.9 %collective-permute-start.4 = (bf16[6,2,384,128]{3,2,1,0:T(8,128)(2,1)S(1)}, bf16[6,2,384,128]{3,2,1,0:T(8,128)(2,1)}, u32[]{:S(2)}, u32[]{:S(2)}) collective-permute-start(bf16[6,2,384,128]{3,2,1,0:T(8,128)(2,1)S(1)} %join.7.refs_1_), channel_id=1, source_target_pairs={{0,16},{16,0},{32,48},{48,32},{64,80},{80,64},{96,112},{112,96},{1... | collective-permute-start | bytes 3538952 | tf_op jit(solution)/shard_map/ppermute | solution.py:41
  58.4 1.5 %collective-permute-done.9 = bf16[3,4,384,128]{3,2,1,0:T(8,128)(2,1)} collective-permute-done((bf16[3,4,384,128]{3,2,1,0:T(8,128)(2,1)S(1)}, bf16[3,4,384,128]{3,2,1,0:T(8,128)(2,1)}, u32[]{:S(2)}, u32[]{:S(2)}) %collective-permute-start.9) | collective-permute-done | bytes 1179680 | tf_op jit(solution)/shard_map/ppermute | solution.py:41
  59.9 8.8 %collective-permute-start.10 = (bf16[1,2,384,128]{3,2,1,0:T(8,128)(2,1)S(1)}, bf16[1,2,384,128]{3,2,1,0:T(8,128)(2,1)S(1)}, u32[]{:S(2)}, u32[]{:S(2)}) collective-permute-start(bf16[1,2,384,128]{3,2,1,0:T(8,128)(2,1)S(1)} %last_two.1), channel_id=1, source_target_pairs={{0,128},{128,0},{256,384},{384,256},{1,129},{129,1},{257,385},{385... | collective-permute-start | bytes 589832 | tf_op jit(solution)/shard_map/ppermute | solution.py:41
  68.7 4.3 %forward_near.1 = (f32[384,128]{1,0:T(8,128)S(1)}, f32[384,128]{1,0:T(8,128)S(1)}, f32[384,128]{1,0:T(8,128)S(1)}) custom-call(s32[54]{0:T(128)S(1)} %pad_add_fusion.flags, bf16[384,128]{1,0:T(8,128)(2,1)S(1)} %bitcast.51, bf16[3,1536,128]{2,1,0:T(8,128)(2,1)S(1)} %bitcast.43, bf16[3,1536,128]{2,1,0:T(8,128)(2,1)} %bitcast.17.n1, ...), custom_call_target="tpu_custom_call" | custom-call | flops 4076863488 | bytes 5308416 | tf_op jit(solution)/shard_map/forward_near/pallas_call | solution.py:317
  73.0 4.3 %forward_rest.1 = (bf16[384,128]{1,0:T(8,128)(2,1)}, bf16[32,128]{1,0:T(8,128)(2,1)S(1)}, f32[384,128]{1,0:T(8,128)S(1)}, f32[384,128]{1,0:T(8,128)S(1)}) custom-call(s32[54]{0:T(128)S(1)} %pad_add_fusion.flags, bf16[384,128]{1,0:T(8,128)(2,1)S(1)} %bitcast.52, bf16[384,128]{1,0:T(8,128)(2,1)S(1)} %bitcast.55, bf16[6,768,128]{2,1,0:T(8,128)(2,1)S(1)} %bitcast.37, ...), custom_call_target="tpu_custom_call" | custom-call | flops 4076863488 | bytes 5308416 | tf_op jit(solution)/shard_map/forward_rest/pallas_call | solution.py:317
  78.0 9.8 %collective-permute-start.11 = (bf16[32,128]{1,0:T(8,128)(2,1)S(1)}, bf16[32,128]{1,0:T(8,128)(2,1)S(1)}, u32[]{:S(2)}, u32[]{:S(2)}) collective-permute-start(bf16[32,128]{1,0:T(8,128)(2,1)S(1)} %get-tuple-element.19.refs_4_), channel_id=1, source_target_pairs={{0,128},{128,0},{256,384},{384,256},{1,129},{129,1},{257,385},{385... | collective-permute-start | bytes 24584 | tf_op jit(solution)/shard_map/ppermute | solution.py:41
  88.9 1.9 %collective-permute-start.17 = (bf16[1632,128]{1,0:T(8,128)(2,1)S(1)}, bf16[1632,128]{1,0:T(8,128)(2,1)S(1)}, u32[]{:S(2)}, u32[]{:S(2)}) collective-permute-start(bf16[1632,128]{1,0:T(8,128)(2,1)S(1)} %join.10.l0), channel_id=1, source_target_pairs={{1,2},{2,1},{3,4},{4,3},{5,6},{6,5},{7,8},{8,7},{9,10},{10,9},{11,... | collective-permute-start | bytes 1253384 | tf_op jit(solution)/shard_map/ppermute | solution.py:41
  90.9 1.9 %collective-permute-start.16 = (bf16[1632,128]{1,0:T(8,128)(2,1)S(1)}, bf16[1632,128]{1,0:T(8,128)(2,1)S(1)}, u32[]{:S(2)}, u32[]{:S(2)}) collective-permute-start(bf16[1632,128]{1,0:T(8,128)(2,1)S(1)} %join.10.l0), channel_id=1, source_target_pairs={{0,1},{1,0},{2,3},{3,2},{4,5},{5,4},{6,7},{7,6},{8,9},{9,8},{10,11... | collective-permute-start | bytes 1253384 | tf_op jit(solution)/shard_map/ppermute | solution.py:41
  92.8 8.3 %collective-permute-start.15 = (bf16[1632,128]{1,0:T(8,128)(2,1)S(1)}, bf16[1632,128]{1,0:T(8,128)(2,1)S(1)}, u32[]{:S(2)}, u32[]{:S(2)}) collective-permute-start(bf16[1632,128]{1,0:T(8,128)(2,1)S(1)} %join.10.l0), channel_id=1, source_target_pairs={{16,32},{32,16},{48,64},{64,48},{80,96},{96,80},{17,33},{33,17},{4... | collective-permute-start | bytes 1253384 | tf_op jit(solution)/shard_map/ppermute | solution.py:41
  101.1 1.9 %collective-permute-start.14 = (bf16[1632,128]{1,0:T(8,128)(2,1)S(1)}, bf16[1632,128]{1,0:T(8,128)(2,1)S(1)}, u32[]{:S(2)}, u32[]{:S(2)}) collective-permute-start(bf16[1632,128]{1,0:T(8,128)(2,1)S(1)} %join.10.l0), channel_id=1, source_target_pairs={{0,16},{16,0},{32,48},{48,32},{64,80},{80,64},{96,112},{112,96},{1... | collective-permute-start | bytes 1253384 | tf_op jit(solution)/shard_map/ppermute | solution.py:41
  103.8 3.0 %collective-permute-done.15.refs_3_.l2 = bf16[1632,128]{1,0:T(8,128)(2,1)S(1)} collective-permute-done((bf16[1632,128]{1,0:T(8,128)(2,1)S(1)}, bf16[1632,128]{1,0:T(8,128)(2,1)S(1)}, u32[]{:S(2)}, u32[]{:S(2)}) %collective-permute-start.15) | collective-permute-done | bytes 417824 | tf_op jit(solution)/shard_map/ppermute | solution.py:41
  106.9 4.0 %collective-permute-start.19 = (bf16[2,1632,128]{2,1,0:T(8,128)(2,1)S(1)}, bf16[2,1632,128]{2,1,0:T(8,128)(2,1)S(1)}, u32[]{:S(2)}, u32[]{:S(2)}) collective-permute-start(bf16[2,1632,128]{2,1,0:T(8,128)(2,1)S(1)} %join.11.m0), channel_id=1, source_target_pairs={{16,32},{32,16},{48,64},{64,48},{80,96},{96,80},{17,33},{33,17},{4... | collective-permute-start | bytes 2506760 | tf_op jit(solution)/shard_map/ppermute | solution.py:41
  110.8 1.9 %collective-permute-start.18 = (bf16[2,1632,128]{2,1,0:T(8,128)(2,1)S(1)}, bf16[2,1632,128]{2,1,0:T(8,128)(2,1)S(1)}, u32[]{:S(2)}, u32[]{:S(2)}) collective-permute-start(bf16[2,1632,128]{2,1,0:T(8,128)(2,1)S(1)} %join.11.m0), channel_id=1, source_target_pairs={{0,16},{16,0},{32,48},{48,32},{64,80},{80,64},{96,112},{112,96},{1... | collective-permute-start | bytes 2506760 | tf_op jit(solution)/shard_map/ppermute | solution.py:41
  112.8 6.7 %query_side.1 = bf16[384,128]{1,0:T(8,128)(2,1)} custom-call(s32[54]{0:T(128)S(1)} %pad_add_fusion.flags, bf16[384,128]{1,0:T(8,128)(2,1)S(1)} %bitcast.53, bf16[384,128]{1,0:T(8,128)(2,1)S(1)} %bitcast.56, f32[384,128]{1,0:T(8,128)S(1)} %get-tuple-element.17.norm_ref, f32[384,128]{1,0:T(8,128)S(1)} %get-tuple-element.18.delta_ref, ...), custom_call_target="tpu_custom_call" | custom-call | flops 4076863488 | bytes 5308416 | tf_op jit(solution)/shard_map/query_side/pallas_call | solution.py:317
  121.0 7.2 %key_side.1 = (bf16[384,128]{1,0:T(8,128)(2,1)}, bf16[384,128]{1,0:T(8,128)(2,1)}) custom-call(s32[54]{0:T(128)S(1)} %pad_add_fusion.flags, bf16[384,128]{1,0:T(8,128)(2,1)S(1)} %bitcast.60, bf16[384,128]{1,0:T(8,128)(2,1)S(1)} %bitcast.58, bf16[3,1536,128]{2,1,0:T(8,128)(2,1)S(1)} %bitcast.45, bf16[1632,128]{1,0:T(8,128)(2,1)S(1)} %join.10.l0, ...), custom_call_target="tpu_custom_call" | custom-call | flops 4076863488 | bytes 5308416 | tf_op jit(solution)/shard_map/key_side/pallas_call | solution.py:317
  (79 shorter events, 11.6 us)
Async XLA Ops:
  0.6 25.7 %copy-start.7 = (s32[27,3]{0,1:T(4,128)S(1)}, s32[27,3]{0,1:T(4,128)}, u32[]{:S(2)}) copy-start(s32[27,3]{0,1:T(4,128)} %constant.79) | copy-start | bytes 976
  0.6 25.8 %copy-start.10 = (s32[27]{0:T(128)S(1)}, s32[27]{0:T(128)}, u32[]{:S(2)}) copy-start(s32[27]{0:T(128)} %constant.71.clone) | copy-start | bytes 328
  0.7 25.8 %copy-start.11 = (s32[27]{0:T(128)S(1)}, s32[27]{0:T(128)}, u32[]{:S(2)}) copy-start(s32[27]{0:T(128)} %constant.70.clone) | copy-start | bytes 328
  0.7 25.8 %copy-start.12 = (s32[27]{0:T(128)S(1)}, s32[27]{0:T(128)}, u32[]{:S(2)}) copy-start(s32[27]{0:T(128)} %constant.69.clone) | copy-start | bytes 328
  1.7 24.8 %collective-permute-start.1 = (bf16[1,2,384,128]{3,2,1,0:T(8,128)(2,1)S(1)}, bf16[1,2,384,128]{3,2,1,0:T(8,128)(2,1)S(1)}, u32[]{:S(2)}, u32[]{:S(2)}) collective-permute-start(bf16[1,2,384,128]{3,2,1,0:T(8,128)(2,1)S(1)} %get-tuple-element.27), channel_id=1, source_target_pairs={{128,256},{256,128},{129,257},{257,129},{130,258},{258,130},{131,2... | collective-permute-start | bytes 589832 | tf_op jit(solution)/shard_map/ppermute | solution.py:41
  2.4 32.7 %collective-permute-start = (bf16[1,2,384,128]{3,2,1,0:T(8,128)(2,1)S(1)}, bf16[1,2,384,128]{3,2,1,0:T(8,128)(2,1)S(1)}, u32[]{:S(2)}, u32[]{:S(2)}) collective-permute-start(bf16[1,2,384,128]{3,2,1,0:T(8,128)(2,1)S(1)} %get-tuple-element.27), channel_id=1, source_target_pairs={{0,128},{128,0},{256,384},{384,256},{1,129},{129,1},{257,385},{385... | collective-permute-start | bytes 589832 | tf_op jit(solution)/shard_map/ppermute | solution.py:41
  21.2 18.6 %collective-permute-start.7 = (bf16[1,4,384,128]{3,2,1,0:T(8,128)(2,1)S(1)}, bf16[1,4,384,128]{3,2,1,0:T(8,128)(2,1)S(1)}, u32[]{:S(2)}, u32[]{:S(2)}) collective-permute-start(bf16[1,4,384,128]{3,2,1,0:T(8,128)(2,1)S(1)} %bitcast.39), channel_id=1, source_target_pairs={{1,2},{2,1},{3,4},{4,3},{5,6},{6,5},{7,8},{8,7},{9,10},{10,9},{11,... | collective-permute-start | bytes 1179656 | tf_op jit(solution)/shard_map/ppermute | solution.py:41
  23.7 16.0 %collective-permute-start.6 = (bf16[1,4,384,128]{3,2,1,0:T(8,128)(2,1)S(1)}, bf16[1,4,384,128]{3,2,1,0:T(8,128)(2,1)S(1)}, u32[]{:S(2)}, u32[]{:S(2)}) collective-permute-start(bf16[1,4,384,128]{3,2,1,0:T(8,128)(2,1)S(1)} %bitcast.40), channel_id=1, source_target_pairs={{0,1},{1,0},{2,3},{3,2},{4,5},{5,4},{6,7},{7,6},{8,9},{9,8},{10,11... | collective-permute-start | bytes 1179656 | tf_op jit(solution)/shard_map/ppermute | solution.py:41
  35.1 13.6 %collective-permute-start.3 = (bf16[2,2,384,128]{3,2,1,0:T(8,128)(2,1)S(1)}, bf16[2,2,384,128]{3,2,1,0:T(8,128)(2,1)S(1)}, u32[]{:S(2)}, u32[]{:S(2)}) collective-permute-start(bf16[2,2,384,128]{3,2,1,0:T(8,128)(2,1)S(1)} %join.6.refs_0_), channel_id=1, source_target_pairs={{1,2},{2,1},{3,4},{4,3},{5,6},{6,5},{7,8},{8,7},{9,10},{10,9},{11,... | collective-permute-start | bytes 1179656 | tf_op jit(solution)/shard_map/ppermute | solution.py:41
  37.0 11.7 %collective-permute-start.2 = (bf16[2,2,384,128]{3,2,1,0:T(8,128)(2,1)S(1)}, bf16[2,2,384,128]{3,2,1,0:T(8,128)(2,1)S(1)}, u32[]{:S(2)}, u32[]{:S(2)}) collective-permute-start(bf16[2,2,384,128]{3,2,1,0:T(8,128)(2,1)S(1)} %join.6.refs_0_), channel_id=1, source_target_pairs={{0,1},{1,0},{2,3},{3,2},{4,5},{5,4},{6,7},{7,6},{8,9},{9,8},{10,11... | collective-permute-start | bytes 1179656 | tf_op jit(solution)/shard_map/ppermute | solution.py:41
  39.9 20.0 %collective-permute-start.9 = (bf16[3,4,384,128]{3,2,1,0:T(8,128)(2,1)S(1)}, bf16[3,4,384,128]{3,2,1,0:T(8,128)(2,1)}, u32[]{:S(2)}, u32[]{:S(2)}) collective-permute-start(bf16[3,4,384,128]{3,2,1,0:T(8,128)(2,1)S(1)} %join.9), channel_id=1, source_target_pairs={{16,32},{32,16},{48,64},{64,48},{80,96},{96,80},{17,33},{33,17},{4... | collective-permute-start | bytes 3538952 | tf_op jit(solution)/shard_map/ppermute | solution.py:41
  45.9 22.8 %collective-permute-start.8 = (bf16[3,4,384,128]{3,2,1,0:T(8,128)(2,1)S(1)}, bf16[3,4,384,128]{3,2,1,0:T(8,128)(2,1)}, u32[]{:S(2)}, u32[]{:S(2)}) collective-permute-start(bf16[3,4,384,128]{3,2,1,0:T(8,128)(2,1)S(1)} %join.9), channel_id=1, source_target_pairs={{0,16},{16,0},{32,48},{48,32},{64,80},{80,64},{96,112},{112,96},{1... | collective-permute-start | bytes 3538952 | tf_op jit(solution)/shard_map/ppermute | solution.py:41
  48.9 24.2 %collective-permute-start.5 = (bf16[6,2,384,128]{3,2,1,0:T(8,128)(2,1)S(1)}, bf16[6,2,384,128]{3,2,1,0:T(8,128)(2,1)}, u32[]{:S(2)}, u32[]{:S(2)}) collective-permute-start(bf16[6,2,384,128]{3,2,1,0:T(8,128)(2,1)S(1)} %join.7.refs_1_), channel_id=1, source_target_pairs={{16,32},{32,16},{48,64},{64,48},{80,96},{96,80},{17,33},{33,17},{4... | collective-permute-start | bytes 3538952 | tf_op jit(solution)/shard_map/ppermute | solution.py:41
  54.0 19.0 %collective-permute-start.4 = (bf16[6,2,384,128]{3,2,1,0:T(8,128)(2,1)S(1)}, bf16[6,2,384,128]{3,2,1,0:T(8,128)(2,1)}, u32[]{:S(2)}, u32[]{:S(2)}) collective-permute-start(bf16[6,2,384,128]{3,2,1,0:T(8,128)(2,1)S(1)} %join.7.refs_1_), channel_id=1, source_target_pairs={{0,16},{16,0},{32,48},{48,32},{64,80},{80,64},{96,112},{112,96},{1... | collective-permute-start | bytes 3538952 | tf_op jit(solution)/shard_map/ppermute | solution.py:41
  57.7 30.2 %collective-permute-start.12 = (bf16[1,2,384,128]{3,2,1,0:T(8,128)(2,1)S(1)}, bf16[1,2,384,128]{3,2,1,0:T(8,128)(2,1)S(1)}, u32[]{:S(2)}, u32[]{:S(2)}) collective-permute-start(bf16[1,2,384,128]{3,2,1,0:T(8,128)(2,1)S(1)} %last_two.1), channel_id=1, source_target_pairs={{128,256},{256,128},{129,257},{257,129},{130,258},{258,130},{131,2... | collective-permute-start | bytes 589832 | tf_op jit(solution)/shard_map/ppermute | solution.py:41
  59.9 28.0 %collective-permute-start.10 = (bf16[1,2,384,128]{3,2,1,0:T(8,128)(2,1)S(1)}, bf16[1,2,384,128]{3,2,1,0:T(8,128)(2,1)S(1)}, u32[]{:S(2)}, u32[]{:S(2)}) collective-permute-start(bf16[1,2,384,128]{3,2,1,0:T(8,128)(2,1)S(1)} %last_two.1), channel_id=1, source_target_pairs={{0,128},{128,0},{256,384},{384,256},{1,129},{129,1},{257,385},{385... | collective-permute-start | bytes 589832 | tf_op jit(solution)/shard_map/ppermute | solution.py:41
  77.4 10.5 %collective-permute-start.13 = (bf16[32,128]{1,0:T(8,128)(2,1)S(1)}, bf16[32,128]{1,0:T(8,128)(2,1)S(1)}, u32[]{:S(2)}, u32[]{:S(2)}) collective-permute-start(bf16[32,128]{1,0:T(8,128)(2,1)S(1)} %get-tuple-element.19.refs_4_), channel_id=1, source_target_pairs={{128,256},{256,128},{129,257},{257,129},{130,258},{258,130},{131,2... | collective-permute-start | bytes 24584 | tf_op jit(solution)/shard_map/ppermute | solution.py:41
  78.0 10.9 %collective-permute-start.11 = (bf16[32,128]{1,0:T(8,128)(2,1)S(1)}, bf16[32,128]{1,0:T(8,128)(2,1)S(1)}, u32[]{:S(2)}, u32[]{:S(2)}) collective-permute-start(bf16[32,128]{1,0:T(8,128)(2,1)S(1)} %get-tuple-element.19.refs_4_), channel_id=1, source_target_pairs={{0,128},{128,0},{256,384},{384,256},{1,129},{129,1},{257,385},{385... | collective-permute-start | bytes 24584 | tf_op jit(solution)/shard_map/ppermute | solution.py:41
  88.9 14.7 %collective-permute-start.17 = (bf16[1632,128]{1,0:T(8,128)(2,1)S(1)}, bf16[1632,128]{1,0:T(8,128)(2,1)S(1)}, u32[]{:S(2)}, u32[]{:S(2)}) collective-permute-start(bf16[1632,128]{1,0:T(8,128)(2,1)S(1)} %join.10.l0), channel_id=1, source_target_pairs={{1,2},{2,1},{3,4},{4,3},{5,6},{6,5},{7,8},{8,7},{9,10},{10,9},{11,... | collective-permute-start | bytes 1253384 | tf_op jit(solution)/shard_map/ppermute | solution.py:41
  90.9 12.9 %collective-permute-start.16 = (bf16[1632,128]{1,0:T(8,128)(2,1)S(1)}, bf16[1632,128]{1,0:T(8,128)(2,1)S(1)}, u32[]{:S(2)}, u32[]{:S(2)}) collective-permute-start(bf16[1632,128]{1,0:T(8,128)(2,1)S(1)} %join.10.l0), channel_id=1, source_target_pairs={{0,1},{1,0},{2,3},{3,2},{4,5},{5,4},{6,7},{7,6},{8,9},{9,8},{10,11... | collective-permute-start | bytes 1253384 | tf_op jit(solution)/shard_map/ppermute | solution.py:41
  92.8 14.0 %collective-permute-start.15 = (bf16[1632,128]{1,0:T(8,128)(2,1)S(1)}, bf16[1632,128]{1,0:T(8,128)(2,1)S(1)}, u32[]{:S(2)}, u32[]{:S(2)}) collective-permute-start(bf16[1632,128]{1,0:T(8,128)(2,1)S(1)} %join.10.l0), channel_id=1, source_target_pairs={{16,32},{32,16},{48,64},{64,48},{80,96},{96,80},{17,33},{33,17},{4... | collective-permute-start | bytes 1253384 | tf_op jit(solution)/shard_map/ppermute | solution.py:41
  101.1 5.7 %collective-permute-start.14 = (bf16[1632,128]{1,0:T(8,128)(2,1)S(1)}, bf16[1632,128]{1,0:T(8,128)(2,1)S(1)}, u32[]{:S(2)}, u32[]{:S(2)}) collective-permute-start(bf16[1632,128]{1,0:T(8,128)(2,1)S(1)} %join.10.l0), channel_id=1, source_target_pairs={{0,16},{16,0},{32,48},{48,32},{64,80},{80,64},{96,112},{112,96},{1... | collective-permute-start | bytes 1253384 | tf_op jit(solution)/shard_map/ppermute | solution.py:41
  106.9 14.2 %collective-permute-start.19 = (bf16[2,1632,128]{2,1,0:T(8,128)(2,1)S(1)}, bf16[2,1632,128]{2,1,0:T(8,128)(2,1)S(1)}, u32[]{:S(2)}, u32[]{:S(2)}) collective-permute-start(bf16[2,1632,128]{2,1,0:T(8,128)(2,1)S(1)} %join.11.m0), channel_id=1, source_target_pairs={{16,32},{32,16},{48,64},{64,48},{80,96},{96,80},{17,33},{33,17},{4... | collective-permute-start | bytes 2506760 | tf_op jit(solution)/shard_map/ppermute | solution.py:41
  110.8 10.2 %collective-permute-start.18 = (bf16[2,1632,128]{2,1,0:T(8,128)(2,1)S(1)}, bf16[2,1632,128]{2,1,0:T(8,128)(2,1)S(1)}, u32[]{:S(2)}, u32[]{:S(2)}) collective-permute-start(bf16[2,1632,128]{2,1,0:T(8,128)(2,1)S(1)} %join.11.m0), channel_id=1, source_target_pairs={{0,16},{16,0},{32,48},{48,32},{64,80},{80,64},{96,112},{112,96},{1... | collective-permute-start | bytes 2506760 | tf_op jit(solution)/shard_map/ppermute | solution.py:41
  (9 other events, 105.7 us)

commit v3 on v2

--- a/solution.py
+++ b/solution.py
@@ -19,7 +19,8 @@
 LINE_ROWS = 2 * BLOCK_ROWS + STAT_ROWS
 NEAR_GROUP = 4
 REST_GROUP = 5
-BACKWARD_GROUP = 3
+BACKWARD_GROUP = 6
+BACKWARD_TAIL = 3
 MASKED = 1e30
 VMEM_LIMIT = 24 * 1024 * 1024
 JOIN_LIMIT = 8 * 1024 * 1024
@@ -130,11 +131,11 @@
     del at
 
 
-def each_group(number, size, wait, step):
-    def body(group, carry):
+def each_group(number, size, wait, step, tail=None):
+    def run(first, count):
         blocks, biases = [], []
-        for k in range(size):
-            at = group * size + k
+        for k in range(count):
+            at = first + k
 
             @pl.when(at < number)
             def _(at=at):
@@ -143,9 +144,20 @@
             blocks.append(jnp.minimum(at, number - 1))
             biases.append(jnp.where(at < number, 0.0, MASKED).astype(jnp.float32))
         step(blocks, biases)
+
+    def body(group, carry):
+        run(group * size, size)
         return carry
 
-    lax.fori_loop(0, lax.div(number + size - 1, size), body, 0)
+    if tail is None:
+        lax.fori_loop(0, lax.div(number + size - 1, size), body, 0)
+        return
+    whole = lax.div(number + size - tail - 1, size)
+    lax.fori_loop(0, whole, body, 0)
+
+    @pl.when(whole * size < number)
+    def _():
+        run(whole * size, tail)
 
 
 def forward_groups(number, size, wait, q_ref, kv, peak, total, acc):
@@ -236,7 +248,7 @@
             sum_of = sum_of + matmul(jnp.concatenate(parts, axis=1), kv[block, :ROWS], NN_DIMS)
         acc[...] = sum_of
 
-    each_group(number, BACKWARD_GROUP, wait, step)
+    each_group(number, BACKWARD_GROUP, wait, step, BACKWARD_TAIL)
     out_ref[...] = acc[...].astype(out_ref.dtype)
 
 
@@ -302,7 +314,7 @@
         key_acc[...] = key_sum
         value_acc[...] = value_sum
 
-    each_group(number, BACKWARD_GROUP, no_wait, step)
+    each_group(number, BACKWARD_GROUP, no_wait, step, BACKWARD_TAIL)
     key_out[...] = (key_acc[...] * SCALE).astype(key_out.dtype)
     value_out[...] = value_acc[...].astype(value_out.dtype)
 

time: 131 us -> 129 us (0.985)
  Pallas kernels: 22.9 us -> 20.9 us
    pallas_call x4, Pallas kernels: 22.6 us -> 20.6 us  [run(): pl.pallas_call(kernel, out_shape=out_shape, in_specs=[smem] + [anywhere i...]
  transfers between devices with their start and end apart: 20 -> 20, of which waited for: 8 -> 7; matrix products, arithmetic and copies ran while one was open for 2% -> 2% of each run, Pallas kernels for 12% -> 12%
where the time goes in v3:
time: 129 us; the launch traced here: 127 us
  starting transfers between devices  81.5 us (63%)
  Pallas kernels  20.9 us (16%)
  waiting for transfers between devices  17.9 us (14%)
  local copies, waits for them, and re-layouts  3.35 us (3%)
  other arithmetic  1.92 us (1%)
  between operations  1.33 us (1%)
    ppermute x20, starting transfers between devices, swap(): results.append(lax.ppermute(value, axis, pairs))  81.5 us
    pallas_call x4, Pallas kernels, run(): pl.pallas_call(kernel, out_shape=out_shape, in_specs=[smem] + [anywhere i...  20.6 us
    ppermute x20, waiting for transfers between devices, swap(): results.append(lax.ppermute(value, axis, pairs))  17.9 us
  transfers between devices with their start and end apart: 20, of which 7 were waited for; matrix products, arithmetic and copies ran while one was open for 2% of the time, Pallas kernels for 12%

profile of v3, /device:TPU:7, one launch (start us, length us, event | category | flops | bytes accessed | tf_op | source)
XLA Modules:
  0.0 126.9 jit_solution(12103409190905502294)
XLA Ops:
  2.4 17.0 %collective-permute-start = (bf16[1,2,384,128]{3,2,1,0:T(8,128)(2,1)S(1)}, bf16[1,2,384,128]{3,2,1,0:T(8,128)(2,1)S(1)}, u32[]{:S(2)}, u32[]{:S(2)}) collective-permute-start(bf16[1,2,384,128]{3,2,1,0:T(8,128)(2,1)S(1)} %get-tuple-element.27), channel_id=1, source_target_pairs={{0,128},{128,0},{256,384},{384,256},{1,129},{129,1},{257,385},{385... | collective-permute-start | bytes 589832 | tf_op jit(solution)/shard_map/ppermute | solution.py:42
  21.2 2.6 %collective-permute-start.7 = (bf16[1,4,384,128]{3,2,1,0:T(8,128)(2,1)S(1)}, bf16[1,4,384,128]{3,2,1,0:T(8,128)(2,1)S(1)}, u32[]{:S(2)}, u32[]{:S(2)}) collective-permute-start(bf16[1,4,384,128]{3,2,1,0:T(8,128)(2,1)S(1)} %bitcast.39), channel_id=1, source_target_pairs={{1,2},{2,1},{3,4},{4,3},{5,6},{6,5},{7,8},{8,7},{9,10},{10,9},{11,... | collective-permute-start | bytes 1179656 | tf_op jit(solution)/shard_map/ppermute | solution.py:42
  23.7 2.1 %collective-permute-start.6 = (bf16[1,4,384,128]{3,2,1,0:T(8,128)(2,1)S(1)}, bf16[1,4,384,128]{3,2,1,0:T(8,128)(2,1)S(1)}, u32[]{:S(2)}, u32[]{:S(2)}) collective-permute-start(bf16[1,4,384,128]{3,2,1,0:T(8,128)(2,1)S(1)} %bitcast.40), channel_id=1, source_target_pairs={{0,1},{1,0},{2,3},{3,2},{4,5},{5,4},{6,7},{7,6},{8,9},{9,8},{10,11... | collective-permute-start | bytes 1179656 | tf_op jit(solution)/shard_map/ppermute | solution.py:42
  26.5 8.6 %collective-permute-done.refs_0_ = bf16[1,2,384,128]{3,2,1,0:T(8,128)(2,1)S(1)} collective-permute-done((bf16[1,2,384,128]{3,2,1,0:T(8,128)(2,1)S(1)}, bf16[1,2,384,128]{3,2,1,0:T(8,128)(2,1)S(1)}, u32[]{:S(2)}, u32[]{:S(2)}) %collective-permute-start) | collective-permute-done | bytes 196640 | tf_op jit(solution)/shard_map/ppermute | solution.py:42
  35.1 1.9 %collective-permute-start.3 = (bf16[2,2,384,128]{3,2,1,0:T(8,128)(2,1)S(1)}, bf16[2,2,384,128]{3,2,1,0:T(8,128)(2,1)S(1)}, u32[]{:S(2)}, u32[]{:S(2)}) collective-permute-start(bf16[2,2,384,128]{3,2,1,0:T(8,128)(2,1)S(1)} %join.6.refs_0_), channel_id=1, source_target_pairs={{1,2},{2,1},{3,4},{4,3},{5,6},{6,5},{7,8},{8,7},{9,10},{10,9},{11,... | collective-permute-start | bytes 1179656 | tf_op jit(solution)/shard_map/ppermute | solution.py:42
  37.0 2.7 %collective-permute-start.2 = (bf16[2,2,384,128]{3,2,1,0:T(8,128)(2,1)S(1)}, bf16[2,2,384,128]{3,2,1,0:T(8,128)(2,1)S(1)}, u32[]{:S(2)}, u32[]{:S(2)}) collective-permute-start(bf16[2,2,384,128]{3,2,1,0:T(8,128)(2,1)S(1)} %join.6.refs_0_), channel_id=1, source_target_pairs={{0,1},{1,0},{2,3},{3,2},{4,5},{5,4},{6,7},{7,6},{8,9},{9,8},{10,11... | collective-permute-start | bytes 1179656 | tf_op jit(solution)/shard_map/ppermute | solution.py:42
  39.9 6.1 %collective-permute-start.9 = (bf16[3,4,384,128]{3,2,1,0:T(8,128)(2,1)S(1)}, bf16[3,4,384,128]{3,2,1,0:T(8,128)(2,1)}, u32[]{:S(2)}, u32[]{:S(2)}) collective-permute-start(bf16[3,4,384,128]{3,2,1,0:T(8,128)(2,1)S(1)} %join.9), channel_id=1, source_target_pairs={{16,32},{32,16},{48,64},{64,48},{80,96},{96,80},{17,33},{33,17},{4... | collective-permute-start | bytes 3538952 | tf_op jit(solution)/shard_map/ppermute | solution.py:42
  45.9 1.9 %collective-permute-start.8 = (bf16[3,4,384,128]{3,2,1,0:T(8,128)(2,1)S(1)}, bf16[3,4,384,128]{3,2,1,0:T(8,128)(2,1)}, u32[]{:S(2)}, u32[]{:S(2)}) collective-permute-start(bf16[3,4,384,128]{3,2,1,0:T(8,128)(2,1)S(1)} %join.9), channel_id=1, source_target_pairs={{0,16},{16,0},{32,48},{48,32},{64,80},{80,64},{96,112},{112,96},{1... | collective-permute-start | bytes 3538952 | tf_op jit(solution)/shard_map/ppermute | solution.py:42
  48.9 5.1 %collective-permute-start.5 = (bf16[6,2,384,128]{3,2,1,0:T(8,128)(2,1)S(1)}, bf16[6,2,384,128]{3,2,1,0:T(8,128)(2,1)}, u32[]{:S(2)}, u32[]{:S(2)}) collective-permute-start(bf16[6,2,384,128]{3,2,1,0:T(8,128)(2,1)S(1)} %join.7.refs_1_), channel_id=1, source_target_pairs={{16,32},{32,16},{48,64},{64,48},{80,96},{96,80},{17,33},{33,17},{4... | collective-permute-start | bytes 3538952 | tf_op jit(solution)/shard_map/ppermute | solution.py:42
  54.0 1.9 %collective-permute-start.4 = (bf16[6,2,384,128]{3,2,1,0:T(8,128)(2,1)S(1)}, bf16[6,2,384,128]{3,2,1,0:T(8,128)(2,1)}, u32[]{:S(2)}, u32[]{:S(2)}) collective-permute-start(bf16[6,2,384,128]{3,2,1,0:T(8,128)(2,1)S(1)} %join.7.refs_1_), channel_id=1, source_target_pairs={{0,16},{16,0},{32,48},{48,32},{64,80},{80,64},{96,112},{112,96},{1... | collective-permute-start | bytes 3538952 | tf_op jit(solution)/shard_map/ppermute | solution.py:42
  59.9 8.8 %collective-permute-start.10 = (bf16[1,2,384,128]{3,2,1,0:T(8,128)(2,1)S(1)}, bf16[1,2,384,128]{3,2,1,0:T(8,128)(2,1)S(1)}, u32[]{:S(2)}, u32[]{:S(2)}) collective-permute-start(bf16[1,2,384,128]{3,2,1,0:T(8,128)(2,1)S(1)} %last_two.1), channel_id=1, source_target_pairs={{0,128},{128,0},{256,384},{384,256},{1,129},{129,1},{257,385},{385... | collective-permute-start | bytes 589832 | tf_op jit(solution)/shard_map/ppermute | solution.py:42
  68.7 4.3 %forward_near.1 = (f32[384,128]{1,0:T(8,128)S(1)}, f32[384,128]{1,0:T(8,128)S(1)}, f32[384,128]{1,0:T(8,128)S(1)}) custom-call(s32[54]{0:T(128)S(1)} %pad_add_fusion.flags, bf16[384,128]{1,0:T(8,128)(2,1)S(1)} %bitcast.51, bf16[3,1536,128]{2,1,0:T(8,128)(2,1)S(1)} %bitcast.43, bf16[3,1536,128]{2,1,0:T(8,128)(2,1)} %bitcast.17.n1, ...), custom_call_target="tpu_custom_call" | custom-call | flops 4076863488 | bytes 5308416 | tf_op jit(solution)/shard_map/forward_near/pallas_call | solution.py:329
  73.0 4.2 %forward_rest.1 = (bf16[384,128]{1,0:T(8,128)(2,1)}, bf16[32,128]{1,0:T(8,128)(2,1)S(1)}, f32[384,128]{1,0:T(8,128)S(1)}, f32[384,128]{1,0:T(8,128)S(1)}) custom-call(s32[54]{0:T(128)S(1)} %pad_add_fusion.flags, bf16[384,128]{1,0:T(8,128)(2,1)S(1)} %bitcast.52, bf16[384,128]{1,0:T(8,128)(2,1)S(1)} %bitcast.55, bf16[6,768,128]{2,1,0:T(8,128)(2,1)S(1)} %bitcast.37, ...), custom_call_target="tpu_custom_call" | custom-call | flops 4076863488 | bytes 5308416 | tf_op jit(solution)/shard_map/forward_rest/pallas_call | solution.py:329
  77.9 9.9 %collective-permute-start.11 = (bf16[32,128]{1,0:T(8,128)(2,1)S(1)}, bf16[32,128]{1,0:T(8,128)(2,1)S(1)}, u32[]{:S(2)}, u32[]{:S(2)}) collective-permute-start(bf16[32,128]{1,0:T(8,128)(2,1)S(1)} %get-tuple-element.19.refs_4_), channel_id=1, source_target_pairs={{0,128},{128,0},{256,384},{384,256},{1,129},{129,1},{257,385},{385... | collective-permute-start | bytes 24584 | tf_op jit(solution)/shard_map/ppermute | solution.py:42
  89.0 3.2 %collective-permute-start.17 = (bf16[1632,128]{1,0:T(8,128)(2,1)S(1)}, bf16[1632,128]{1,0:T(8,128)(2,1)S(1)}, u32[]{:S(2)}, u32[]{:S(2)}) collective-permute-start(bf16[1632,128]{1,0:T(8,128)(2,1)S(1)} %join.10.l0), channel_id=1, source_target_pairs={{1,2},{2,1},{3,4},{4,3},{5,6},{6,5},{7,8},{8,7},{9,10},{10,9},{11,... | collective-permute-start | bytes 1253384 | tf_op jit(solution)/shard_map/ppermute | solution.py:42
  92.3 1.9 %collective-permute-start.16 = (bf16[1632,128]{1,0:T(8,128)(2,1)S(1)}, bf16[1632,128]{1,0:T(8,128)(2,1)S(1)}, u32[]{:S(2)}, u32[]{:S(2)}) collective-permute-start(bf16[1632,128]{1,0:T(8,128)(2,1)S(1)} %join.10.l0), channel_id=1, source_target_pairs={{0,1},{1,0},{2,3},{3,2},{4,5},{5,4},{6,7},{7,6},{8,9},{9,8},{10,11... | collective-permute-start | bytes 1253384 | tf_op jit(solution)/shard_map/ppermute | solution.py:42
  94.2 6.9 %collective-permute-start.15 = (bf16[1632,128]{1,0:T(8,128)(2,1)S(1)}, bf16[1632,128]{1,0:T(8,128)(2,1)S(1)}, u32[]{:S(2)}, u32[]{:S(2)}) collective-permute-start(bf16[1632,128]{1,0:T(8,128)(2,1)S(1)} %join.10.l0), channel_id=1, source_target_pairs={{16,32},{32,16},{48,64},{64,48},{80,96},{96,80},{17,33},{33,17},{4... | collective-permute-start | bytes 1253384 | tf_op jit(solution)/shard_map/ppermute | solution.py:42
  101.1 1.9 %collective-permute-start.14 = (bf16[1632,128]{1,0:T(8,128)(2,1)S(1)}, bf16[1632,128]{1,0:T(8,128)(2,1)S(1)}, u32[]{:S(2)}, u32[]{:S(2)}) collective-permute-start(bf16[1632,128]{1,0:T(8,128)(2,1)S(1)} %join.10.l0), channel_id=1, source_target_pairs={{0,16},{16,0},{32,48},{48,32},{64,80},{80,64},{96,112},{112,96},{1... | collective-permute-start | bytes 1253384 | tf_op jit(solution)/shard_map/ppermute | solution.py:42
  103.7 3.0 %collective-permute-done.15.refs_3_.l2 = bf16[1632,128]{1,0:T(8,128)(2,1)S(1)} collective-permute-done((bf16[1632,128]{1,0:T(8,128)(2,1)S(1)}, bf16[1632,128]{1,0:T(8,128)(2,1)S(1)}, u32[]{:S(2)}, u32[]{:S(2)}) %collective-permute-start.15) | collective-permute-done | bytes 417824 | tf_op jit(solution)/shard_map/ppermute | solution.py:42
  106.8 3.6 %collective-permute-start.19 = (bf16[2,1632,128]{2,1,0:T(8,128)(2,1)S(1)}, bf16[2,1632,128]{2,1,0:T(8,128)(2,1)S(1)}, u32[]{:S(2)}, u32[]{:S(2)}) collective-permute-start(bf16[2,1632,128]{2,1,0:T(8,128)(2,1)S(1)} %join.11.m0), channel_id=1, source_target_pairs={{16,32},{32,16},{48,64},{64,48},{80,96},{96,80},{17,33},{33,17},{4... | collective-permute-start | bytes 2506760 | tf_op jit(solution)/shard_map/ppermute | solution.py:42
  110.5 1.9 %collective-permute-start.18 = (bf16[2,1632,128]{2,1,0:T(8,128)(2,1)S(1)}, bf16[2,1632,128]{2,1,0:T(8,128)(2,1)S(1)}, u32[]{:S(2)}, u32[]{:S(2)}) collective-permute-start(bf16[2,1632,128]{2,1,0:T(8,128)(2,1)S(1)} %join.11.m0), channel_id=1, source_target_pairs={{0,16},{16,0},{32,48},{48,32},{64,80},{80,64},{96,112},{112,96},{1... | collective-permute-start | bytes 2506760 | tf_op jit(solution)/shard_map/ppermute | solution.py:42
  112.4 6.1 %query_side.1 = bf16[384,128]{1,0:T(8,128)(2,1)} custom-call(s32[54]{0:T(128)S(1)} %pad_add_fusion.flags, bf16[384,128]{1,0:T(8,128)(2,1)S(1)} %bitcast.53, bf16[384,128]{1,0:T(8,128)(2,1)S(1)} %bitcast.56, f32[384,128]{1,0:T(8,128)S(1)} %get-tuple-element.17.norm_ref, f32[384,128]{1,0:T(8,128)S(1)} %get-tuple-element.18.delta_ref, ...), custom_call_target="tpu_custom_call" | custom-call | flops 4076863488 | bytes 5308416 | tf_op jit(solution)/shard_map/query_side/pallas_call | solution.py:329
  118.5 2.1 %collective-permute-done.19.m2 = bf16[2,1632,128]{2,1,0:T(8,128)(2,1)S(1)} collective-permute-done((bf16[2,1632,128]{2,1,0:T(8,128)(2,1)S(1)}, bf16[2,1632,128]{2,1,0:T(8,128)(2,1)S(1)}, u32[]{:S(2)}, u32[]{:S(2)}) %collective-permute-start.19) | collective-permute-done | bytes 835616 | tf_op jit(solution)/shard_map/ppermute | solution.py:42
  120.7 6.0 %key_side.1 = (bf16[384,128]{1,0:T(8,128)(2,1)}, bf16[384,128]{1,0:T(8,128)(2,1)}) custom-call(s32[54]{0:T(128)S(1)} %pad_add_fusion.flags, bf16[384,128]{1,0:T(8,128)(2,1)S(1)} %bitcast.60, bf16[384,128]{1,0:T(8,128)(2,1)S(1)} %bitcast.58, bf16[3,1536,128]{2,1,0:T(8,128)(2,1)S(1)} %bitcast.45, bf16[1632,128]{1,0:T(8,128)(2,1)S(1)} %join.10.l0, ...), custom_call_target="tpu_custom_call" | custom-call | flops 4076863488 | bytes 5308416 | tf_op jit(solution)/shard_map/key_side/pallas_call | solution.py:329
  (79 shorter events, 11.7 us)
Async XLA Ops:
  0.6 25.7 %copy-start.7 = (s32[27,3]{0,1:T(4,128)S(1)}, s32[27,3]{0,1:T(4,128)}, u32[]{:S(2)}) copy-start(s32[27,3]{0,1:T(4,128)} %constant.79) | copy-start | bytes 976
  0.6 25.8 %copy-start.10 = (s32[27]{0:T(128)S(1)}, s32[27]{0:T(128)}, u32[]{:S(2)}) copy-start(s32[27]{0:T(128)} %constant.71.clone) | copy-start | bytes 328
  0.7 25.8 %copy-start.11 = (s32[27]{0:T(128)S(1)}, s32[27]{0:T(128)}, u32[]{:S(2)}) copy-start(s32[27]{0:T(128)} %constant.70.clone) | copy-start | bytes 328
  0.7 25.8 %copy-start.12 = (s32[27]{0:T(128)S(1)}, s32[27]{0:T(128)}, u32[]{:S(2)}) copy-start(s32[27]{0:T(128)} %constant.69.clone) | copy-start | bytes 328
  1.7 24.8 %collective-permute-start.1 = (bf16[1,2,384,128]{3,2,1,0:T(8,128)(2,1)S(1)}, bf16[1,2,384,128]{3,2,1,0:T(8,128)(2,1)S(1)}, u32[]{:S(2)}, u32[]{:S(2)}) collective-permute-start(bf16[1,2,384,128]{3,2,1,0:T(8,128)(2,1)S(1)} %get-tuple-element.27), channel_id=1, source_target_pairs={{128,256},{256,128},{129,257},{257,129},{130,258},{258,130},{131,2... | collective-permute-start | bytes 589832 | tf_op jit(solution)/shard_map/ppermute | solution.py:42
  2.4 32.7 %collective-permute-start = (bf16[1,2,384,128]{3,2,1,0:T(8,128)(2,1)S(1)}, bf16[1,2,384,128]{3,2,1,0:T(8,128)(2,1)S(1)}, u32[]{:S(2)}, u32[]{:S(2)}) collective-permute-start(bf16[1,2,384,128]{3,2,1,0:T(8,128)(2,1)S(1)} %get-tuple-element.27), channel_id=1, source_target_pairs={{0,128},{128,0},{256,384},{384,256},{1,129},{129,1},{257,385},{385... | collective-permute-start | bytes 589832 | tf_op jit(solution)/shard_map/ppermute | solution.py:42
  21.2 18.6 %collective-permute-start.7 = (bf16[1,4,384,128]{3,2,1,0:T(8,128)(2,1)S(1)}, bf16[1,4,384,128]{3,2,1,0:T(8,128)(2,1)S(1)}, u32[]{:S(2)}, u32[]{:S(2)}) collective-permute-start(bf16[1,4,384,128]{3,2,1,0:T(8,128)(2,1)S(1)} %bitcast.39), channel_id=1, source_target_pairs={{1,2},{2,1},{3,4},{4,3},{5,6},{6,5},{7,8},{8,7},{9,10},{10,9},{11,... | collective-permute-start | bytes 1179656 | tf_op jit(solution)/shard_map/ppermute | solution.py:42
  23.7 16.0 %collective-permute-start.6 = (bf16[1,4,384,128]{3,2,1,0:T(8,128)(2,1)S(1)}, bf16[1,4,384,128]{3,2,1,0:T(8,128)(2,1)S(1)}, u32[]{:S(2)}, u32[]{:S(2)}) collective-permute-start(bf16[1,4,384,128]{3,2,1,0:T(8,128)(2,1)S(1)} %bitcast.40), channel_id=1, source_target_pairs={{0,1},{1,0},{2,3},{3,2},{4,5},{5,4},{6,7},{7,6},{8,9},{9,8},{10,11... | collective-permute-start | bytes 1179656 | tf_op jit(solution)/shard_map/ppermute | solution.py:42
  35.1 13.6 %collective-permute-start.3 = (bf16[2,2,384,128]{3,2,1,0:T(8,128)(2,1)S(1)}, bf16[2,2,384,128]{3,2,1,0:T(8,128)(2,1)S(1)}, u32[]{:S(2)}, u32[]{:S(2)}) collective-permute-start(bf16[2,2,384,128]{3,2,1,0:T(8,128)(2,1)S(1)} %join.6.refs_0_), channel_id=1, source_target_pairs={{1,2},{2,1},{3,4},{4,3},{5,6},{6,5},{7,8},{8,7},{9,10},{10,9},{11,... | collective-permute-start | bytes 1179656 | tf_op jit(solution)/shard_map/ppermute | solution.py:42
  37.0 11.7 %collective-permute-start.2 = (bf16[2,2,384,128]{3,2,1,0:T(8,128)(2,1)S(1)}, bf16[2,2,384,128]{3,2,1,0:T(8,128)(2,1)S(1)}, u32[]{:S(2)}, u32[]{:S(2)}) collective-permute-start(bf16[2,2,384,128]{3,2,1,0:T(8,128)(2,1)S(1)} %join.6.refs_0_), channel_id=1, source_target_pairs={{0,1},{1,0},{2,3},{3,2},{4,5},{5,4},{6,7},{7,6},{8,9},{9,8},{10,11... | collective-permute-start | bytes 1179656 | tf_op jit(solution)/shard_map/ppermute | solution.py:42
  39.9 20.0 %collective-permute-start.9 = (bf16[3,4,384,128]{3,2,1,0:T(8,128)(2,1)S(1)}, bf16[3,4,384,128]{3,2,1,0:T(8,128)(2,1)}, u32[]{:S(2)}, u32[]{:S(2)}) collective-permute-start(bf16[3,4,384,128]{3,2,1,0:T(8,128)(2,1)S(1)} %join.9), channel_id=1, source_target_pairs={{16,32},{32,16},{48,64},{64,48},{80,96},{96,80},{17,33},{33,17},{4... | collective-permute-start | bytes 3538952 | tf_op jit(solution)/shard_map/ppermute | solution.py:42
  45.9 22.8 %collective-permute-start.8 = (bf16[3,4,384,128]{3,2,1,0:T(8,128)(2,1)S(1)}, bf16[3,4,384,128]{3,2,1,0:T(8,128)(2,1)}, u32[]{:S(2)}, u32[]{:S(2)}) collective-permute-start(bf16[3,4,384,128]{3,2,1,0:T(8,128)(2,1)S(1)} %join.9), channel_id=1, source_target_pairs={{0,16},{16,0},{32,48},{48,32},{64,80},{80,64},{96,112},{112,96},{1... | collective-permute-start | bytes 3538952 | tf_op jit(solution)/shard_map/ppermute | solution.py:42
  48.9 24.2 %collective-permute-start.5 = (bf16[6,2,384,128]{3,2,1,0:T(8,128)(2,1)S(1)}, bf16[6,2,384,128]{3,2,1,0:T(8,128)(2,1)}, u32[]{:S(2)}, u32[]{:S(2)}) collective-permute-start(bf16[6,2,384,128]{3,2,1,0:T(8,128)(2,1)S(1)} %join.7.refs_1_), channel_id=1, source_target_pairs={{16,32},{32,16},{48,64},{64,48},{80,96},{96,80},{17,33},{33,17},{4... | collective-permute-start | bytes 3538952 | tf_op jit(solution)/shard_map/ppermute | solution.py:42
  54.0 19.1 %collective-permute-start.4 = (bf16[6,2,384,128]{3,2,1,0:T(8,128)(2,1)S(1)}, bf16[6,2,384,128]{3,2,1,0:T(8,128)(2,1)}, u32[]{:S(2)}, u32[]{:S(2)}) collective-permute-start(bf16[6,2,384,128]{3,2,1,0:T(8,128)(2,1)S(1)} %join.7.refs_1_), channel_id=1, source_target_pairs={{0,16},{16,0},{32,48},{48,32},{64,80},{80,64},{96,112},{112,96},{1... | collective-permute-start | bytes 3538952 | tf_op jit(solution)/shard_map/ppermute | solution.py:42
  57.7 30.2 %collective-permute-start.12 = (bf16[1,2,384,128]{3,2,1,0:T(8,128)(2,1)S(1)}, bf16[1,2,384,128]{3,2,1,0:T(8,128)(2,1)S(1)}, u32[]{:S(2)}, u32[]{:S(2)}) collective-permute-start(bf16[1,2,384,128]{3,2,1,0:T(8,128)(2,1)S(1)} %last_two.1), channel_id=1, source_target_pairs={{128,256},{256,128},{129,257},{257,129},{130,258},{258,130},{131,2... | collective-permute-start | bytes 589832 | tf_op jit(solution)/shard_map/ppermute | solution.py:42
  59.9 28.0 %collective-permute-start.10 = (bf16[1,2,384,128]{3,2,1,0:T(8,128)(2,1)S(1)}, bf16[1,2,384,128]{3,2,1,0:T(8,128)(2,1)S(1)}, u32[]{:S(2)}, u32[]{:S(2)}) collective-permute-start(bf16[1,2,384,128]{3,2,1,0:T(8,128)(2,1)S(1)} %last_two.1), channel_id=1, source_target_pairs={{0,128},{128,0},{256,384},{384,256},{1,129},{129,1},{257,385},{385... | collective-permute-start | bytes 589832 | tf_op jit(solution)/shard_map/ppermute | solution.py:42
  77.3 10.6 %collective-permute-start.13 = (bf16[32,128]{1,0:T(8,128)(2,1)S(1)}, bf16[32,128]{1,0:T(8,128)(2,1)S(1)}, u32[]{:S(2)}, u32[]{:S(2)}) collective-permute-start(bf16[32,128]{1,0:T(8,128)(2,1)S(1)} %get-tuple-element.19.refs_4_), channel_id=1, source_target_pairs={{128,256},{256,128},{129,257},{257,129},{130,258},{258,130},{131,2... | collective-permute-start | bytes 24584 | tf_op jit(solution)/shard_map/ppermute | solution.py:42
  77.9 11.0 %collective-permute-start.11 = (bf16[32,128]{1,0:T(8,128)(2,1)S(1)}, bf16[32,128]{1,0:T(8,128)(2,1)S(1)}, u32[]{:S(2)}, u32[]{:S(2)}) collective-permute-start(bf16[32,128]{1,0:T(8,128)(2,1)S(1)} %get-tuple-element.19.refs_4_), channel_id=1, source_target_pairs={{0,128},{128,0},{256,384},{384,256},{1,129},{129,1},{257,385},{385... | collective-permute-start | bytes 24584 | tf_op jit(solution)/shard_map/ppermute | solution.py:42
  89.0 14.7 %collective-permute-start.17 = (bf16[1632,128]{1,0:T(8,128)(2,1)S(1)}, bf16[1632,128]{1,0:T(8,128)(2,1)S(1)}, u32[]{:S(2)}, u32[]{:S(2)}) collective-permute-start(bf16[1632,128]{1,0:T(8,128)(2,1)S(1)} %join.10.l0), channel_id=1, source_target_pairs={{1,2},{2,1},{3,4},{4,3},{5,6},{6,5},{7,8},{8,7},{9,10},{10,9},{11,... | collective-permute-start | bytes 1253384 | tf_op jit(solution)/shard_map/ppermute | solution.py:42
  92.3 11.5 %collective-permute-start.16 = (bf16[1632,128]{1,0:T(8,128)(2,1)S(1)}, bf16[1632,128]{1,0:T(8,128)(2,1)S(1)}, u32[]{:S(2)}, u32[]{:S(2)}) collective-permute-start(bf16[1632,128]{1,0:T(8,128)(2,1)S(1)} %join.10.l0), channel_id=1, source_target_pairs={{0,1},{1,0},{2,3},{3,2},{4,5},{5,4},{6,7},{7,6},{8,9},{9,8},{10,11... | collective-permute-start | bytes 1253384 | tf_op jit(solution)/shard_map/ppermute | solution.py:42
  94.2 12.6 %collective-permute-start.15 = (bf16[1632,128]{1,0:T(8,128)(2,1)S(1)}, bf16[1632,128]{1,0:T(8,128)(2,1)S(1)}, u32[]{:S(2)}, u32[]{:S(2)}) collective-permute-start(bf16[1632,128]{1,0:T(8,128)(2,1)S(1)} %join.10.l0), channel_id=1, source_target_pairs={{16,32},{32,16},{48,64},{64,48},{80,96},{96,80},{17,33},{33,17},{4... | collective-permute-start | bytes 1253384 | tf_op jit(solution)/shard_map/ppermute | solution.py:42
  101.1 5.7 %collective-permute-start.14 = (bf16[1632,128]{1,0:T(8,128)(2,1)S(1)}, bf16[1632,128]{1,0:T(8,128)(2,1)S(1)}, u32[]{:S(2)}, u32[]{:S(2)}) collective-permute-start(bf16[1632,128]{1,0:T(8,128)(2,1)S(1)} %join.10.l0), channel_id=1, source_target_pairs={{0,16},{16,0},{32,48},{48,32},{64,80},{80,64},{96,112},{112,96},{1... | collective-permute-start | bytes 1253384 | tf_op jit(solution)/shard_map/ppermute | solution.py:42
  106.8 13.8 %collective-permute-start.19 = (bf16[2,1632,128]{2,1,0:T(8,128)(2,1)S(1)}, bf16[2,1632,128]{2,1,0:T(8,128)(2,1)S(1)}, u32[]{:S(2)}, u32[]{:S(2)}) collective-permute-start(bf16[2,1632,128]{2,1,0:T(8,128)(2,1)S(1)} %join.11.m0), channel_id=1, source_target_pairs={{16,32},{32,16},{48,64},{64,48},{80,96},{96,80},{17,33},{33,17},{4... | collective-permute-start | bytes 2506760 | tf_op jit(solution)/shard_map/ppermute | solution.py:42
  110.5 10.2 %collective-permute-start.18 = (bf16[2,1632,128]{2,1,0:T(8,128)(2,1)S(1)}, bf16[2,1632,128]{2,1,0:T(8,128)(2,1)S(1)}, u32[]{:S(2)}, u32[]{:S(2)}) collective-permute-start(bf16[2,1632,128]{2,1,0:T(8,128)(2,1)S(1)} %join.11.m0), channel_id=1, source_target_pairs={{0,16},{16,0},{32,48},{48,32},{64,80},{80,64},{96,112},{112,96},{1... | collective-permute-start | bytes 2506760 | tf_op jit(solution)/shard_map/ppermute | solution.py:42
  (9 other events, 105.7 us)
